TPU v7x, 32 devices: a whole 2x2x4 slice. The times are simulated.
32 devices in a mesh: energy: 8 (over y, x, core), space: 4 (over z).
Axes of the slice: x: 2, y: 2, z: 4, core: 2. Of those that a mesh axis runs over, the one named last changes fastest.
Arguments:
- g_upper: bfloat16 [2, 32, 4, 384, 384], P(None, 'energy', 'space'), may hold values from -6 to 6
- p_diag: bfloat16 [2, 32, 4, 384, 384], P(None, 'energy', 'space'), may hold values from -0.8984375 to 0.8984375
- p_upper: bfloat16 [2, 32, 4, 384, 384], P(None, 'energy', 'space'), may hold values from -0.8984375 to 0.8984375
- v_diag: bfloat16 [4, 384, 384], P('space'), may hold values from -0.3125 to 0.3125
- v_upper: bfloat16 [4, 384, 384], P('space'), may hold values from -0.3125 to 0.3125
- v_pattern: int32 [4], P('space'), may hold values from 0 to 1, as said below
- element_present: int32 [4, 48], P('space'), may hold values from 0 to 1, as said below
Outputs:
- sigma_upper: bfloat16 [2, 32, 4, 384, 384], P(None, 'energy', 'space')
Inputs may be any that keep to these rules, and one draw needn't show every extreme that they name: `element_present`: no block row has more than 30 present groups, and some block row has exactly 30. `v_pattern`: the first and the last block row always have their upper block; the others may lack it.
All inputs are finite; a program needn't handle non-finite values.
Results may differ from a plain program's by a relative error of at most 0.013.
Values may be sent and summed in bfloat16 or wider, within the bound.
A program may use at most 128 MiB of HBM per device.

v0:
```python
import math

import jax
import jax.numpy as jnp
from jax import lax
from jax.sharding import PartitionSpec as P

LIVE = 30


def shifted(value, axis, steps):
    count = lax.axis_size(axis)
    pairs = [(source, (source + steps) % count) for source in range(count)]
    return lax.ppermute(value, axis, pairs)


def product(form, left, right):
    return jnp.einsum(form, left, right, preferred_element_type=jnp.float32)


def transform_tables(energies):
    indices = jnp.arange(energies, dtype=jnp.int32)
    phases = indices[:, None] * indices[None, :] % energies
    angles = 2.0 * math.pi / energies * phases.astype(jnp.float32)
    cosine = jnp.cos(angles)
    sine_part = jnp.sin(angles)
    forward = jnp.concatenate(
        [jnp.concatenate([cosine, sine_part], 1), jnp.concatenate([-sine_part, cosine], 1)], 0
    )
    inverse = jnp.concatenate(
        [jnp.concatenate([-sine_part, -cosine], 1), jnp.concatenate([cosine, -sine_part], 1)], 0
    )
    return (forward.astype(jnp.bfloat16), inverse / (energies * math.sqrt(energies)))


def screen(vu_prev, pu_prev, vd_own, pd_own, vu_own, pu_own, pd_next, vd_next, vu_next, pu_next):
    vp_same = (
        product("ki,cekj->ceij", vu_prev, pu_prev)
        + product("ik,cekj->ceij", vd_own, pd_own)
        + product("ik,cejk->ceij", vu_own, pu_own)
    ).astype(jnp.bfloat16)
    vp_one = (
        product("ik,cekj->ceij", vd_own, pu_own) + product("ik,cekj->ceij", vu_own, pd_next)
    ).astype(jnp.bfloat16)
    vp_two = product("ik,cekj->ceij", vu_own, pu_next).astype(jnp.bfloat16)
    total = (
        product("ceik,kj->ceij", vp_same, vu_own)
        + product("ceik,kj->ceij", vp_one, vd_next)
        + product("ceik,jk->ceij", vp_two, vu_next)
    )
    total = total.at[0].add(vu_own.astype(jnp.float32))
    return total.astype(jnp.bfloat16)


def convolve(received):
    green, screened = received
    halves, energies, slots_here, single, columns = green.shape
    forward, inverse = transform_tables(energies)
    flat_cols = slots_here * single * columns

    def spectrum(values):
        return jnp.dot(
            forward,
            values.reshape(halves * energies, flat_cols),
            preferred_element_type=jnp.float32,
        )

    green_freq = spectrum(green)
    screen_freq = spectrum(screened)
    green_re = green_freq[:energies]
    green_im = green_freq[energies:]
    screen_re = screen_freq[:energies]
    screen_im = screen_freq[energies:]
    mixed = jnp.concatenate(
        [green_re * screen_re - green_im * screen_im, green_re * screen_im + green_im * screen_re],
        0,
    )
    result = jnp.dot(inverse, mixed, preferred_element_type=jnp.float32)
    result = result.reshape(halves, energies, slots_here, single, columns).astype(jnp.bfloat16)
    return lax.all_to_all(result, "energy", split_axis=1, concat_axis=3, tiled=True)


def per_device(g_upper, p_diag, p_upper, v_diag, v_upper, v_pattern, element_present):
    peers = lax.axis_size("energy")
    upper_masked = v_upper * v_pattern.astype(jnp.bfloat16)[:, None, None]
    pd_own = p_diag[:, :, 0]
    pu_own = p_upper[:, :, 0]
    vd_own = v_diag[0]
    vu_own = upper_masked[0]
    after_rows = shifted((p_diag, p_upper, v_diag, upper_masked), "space", -1)
    before_rows = shifted((p_upper, upper_masked), "space", 1)
    pd_next = after_rows[0][:, :, 0]
    pu_next = after_rows[1][:, :, 0]
    vd_next = after_rows[2][0]
    vu_next = after_rows[3][0]
    pu_prev = before_rows[0][:, :, 0]
    vu_prev = before_rows[1][0]
    screened = screen(
        vu_prev, pu_prev, vd_own, pd_own, vu_own, pu_own, pd_next, vd_next, vu_next, pu_next
    )
    local_energies = screened.shape[1]
    orbitals = screened.shape[2]
    present_row = element_present[0]
    groups = present_row.shape[0]
    columns = orbitals // groups * orbitals
    live = present_row > 0
    group_ids = jnp.arange(groups, dtype=jnp.int32)
    slots = (LIVE + peers - 1) // peers
    ranking = jnp.cumsum(live.astype(jnp.int32)) - 1
    target = ranking % peers
    slot_of = ranking // peers
    matches = (
        live[:, None, None]
        & (target[:, None, None] == jnp.arange(peers, dtype=jnp.int32)[None, :, None])
        & (slot_of[:, None, None] == jnp.arange(slots, dtype=jnp.int32)[None, None, :])
    )
    source_group = jnp.sum(matches.astype(jnp.int32) * group_ids[:, None, None], axis=0)

    def arrange(values):
        grouped = values.reshape(2, local_energies, groups, columns)
        return jnp.take(grouped, source_group.T, axis=2)

    send_green = arrange(g_upper[:, :, 0])
    send_screen = arrange(screened)
    returned = convolve(
        (
            lax.all_to_all(send_green, "energy", split_axis=3, concat_axis=1, tiled=True),
            lax.all_to_all(send_screen, "energy", split_axis=3, concat_axis=1, tiled=True),
        )
    )
    returned = returned.reshape(2, local_energies, slots * peers, columns)
    picking = jnp.where(live, slot_of * peers + target, 0)
    chosen = jnp.take(returned, picking, axis=2)
    chosen = jnp.where(live[None, None, :, None], chosen, jnp.zeros((), jnp.bfloat16))
    return chosen.reshape(2, local_energies, 1, orbitals, orbitals)


def solution(mesh):
    in_specs = (
        P(None, "energy", "space", None, None),
        P(None, "energy", "space", None, None),
        P(None, "energy", "space", None, None),
        P("space", None, None),
        P("space", None, None),
        P("space"),
        P("space", None),
    )
    out_specs = P(None, "energy", "space", None, None)
    return jax.shard_map(
        per_device, mesh=mesh, in_specs=in_specs, out_specs=out_specs, check_vma=False
    )
```

profile of v0, /device:TPU:0, one launch (start us, length us, event | category | flops | bytes accessed | tf_op | source)
XLA Modules:
  0.0 328.3 jit_solution(13774513346309928541)
XLA Ops:
  0.0 3.0 collective-permute-start.1
  3.0 2.0 collective-permute-start.4
  7.0 3.8 %collective-permute-start.2 = (bf16[2,4,1,384,384]{4,3,1,0,2:T(8,128)(2,1)}, bf16[2,4,1,384,384]{4,3,1,0,2:T(8,128)(2,1)}, u32[]{:S(2)}, u32[]{:S(2)}) collective-permute-start(bf16[2,4,1,384,384]{4,3,1,0,2:T(8,128)(2,1)} %bitcast.169), channel_id=1, source_target_pairs={{0,3},{1,0},{2,1},{3,2},{4,7},{5,4},{6,5},{7,6},{8,11},{9,8},{10,9... | collective-permute-start | bytes 7077896 | tf_op jit(solution)/shard_map/ppermute | solution.py:14
  13.7 5.3 %fusion.18 = f32[384,2,4,384]{3,0,2,1:T(8,128)} fusion(bf16[2,4,1,384,384]{4,3,2,1,0:T(8,128)(2,1)} %param.13, bf16[1,384,384]{1,2,0:T(8,128)(2,1)S(1)} %get-tuple-element.24), kind=kOutput, calls=%fused_computation.25 | convolution fusion | flops 905969664 | bytes 7372800 | tf_op jit(solution)/shard_map/ik,cejk->ceij/dot_general | solution.py:18
  19.3 3.7 %reshape_squeeze.3 = bf16[2,4,48,3072]{3,2,1,0:T(8,128)(2,1)S(1)} reshape(bf16[2,4,1,384,384]{4,3,2,1,0:T(8,128)(2,1)} %param.11) | data formatting | bytes 4718592 | tf_op jit(solution)/shard_map/reshape;squeeze | solution.py:120
  23.0 3.2 copy.79
  26.9 4.8 %gather_fusion.1 = bf16[32,2,4,3072]{3,2,1,0:T(4,128)(2,1)} fusion(bf16[2,4,48,3072]{3,1,2,0:T(4,128)(2,1)} %copy.79, s32[1024]{0:T(1024)S(1)} %pad_clamp_fusion.1), kind=kCustom, calls=%fused_computation.clone | custom fusion | bytes 3145856 | tf_op jit(solution)/shard_map/jit(_take)/gather | solution.py:121
  31.6 3.6 %fusion.20 = f32[2,4,384,384]{2,3,1,0:T(8,128)} fusion(bf16[2,4,1,384,384]{4,3,2,1,0:T(8,128)(2,1)S(1)} %copy-done.1, bf16[1,384,384]{2,1,0:T(8,128)(2,1)S(1)} %copy-done.2), kind=kOutput, calls=%fused_computation.27 | convolution fusion | flops 905969664 | bytes 7372800 | tf_op jit(solution)/shard_map/ik,cekj->ceij/dot_general | solution.py:18
  35.2 79.2 %collective-permute-done = bf16[1,384,384]{1,2,0:T(8,128)(2,1)} collective-permute-done((bf16[1,384,384]{1,2,0:T(8,128)(2,1)S(1)}, bf16[1,384,384]{1,2,0:T(8,128)(2,1)}, u32[]{:S(2)}, u32[]{:S(2)}) %collective-permute-start) | collective-permute-done | bytes 294944 | tf_op jit(solution)/shard_map/ppermute | solution.py:14
  114.4 61.0 %collective-permute-start.5 = (bf16[1,384,384]{1,2,0:T(8,128)(2,1)S(1)}, bf16[1,384,384]{1,2,0:T(8,128)(2,1)}, u32[]{:S(2)}, u32[]{:S(2)}) collective-permute-start(bf16[1,384,384]{1,2,0:T(8,128)(2,1)S(1)} %get-tuple-element.24), channel_id=1, source_target_pairs={{0,3},{1,0},{2,1},{3,2},{4,7},{5,4},{6,5},{7,6},{8,11},{9,8},{10,9... | collective-permute-start | bytes 884744 | tf_op jit(solution)/shard_map/ppermute | solution.py:14
  175.4 9.5 %fusion.5 = f32[2,4,384,384]{3,2,1,0:T(8,128)} fusion(f32[384,2,4,384]{3,0,2,1:T(8,128)} %fusion.18, f32[2,4,384,384]{2,3,1,0:T(8,128)} %fusion.20, bf16[2,4,1,384,384]{4,3,1,0,2:T(8,128)(2,1)} %collective-permute-done.1, bf16[1,384,384]{1,2,0:T(8,128)(2,1)S(1)} %get-tuple-element.24, bf16[1,384,384]{1,2,0:T(8,128)(2,1)} %collective-permute-done), kind=kOutput, calls=%fused_computation.13 | convolution fusion | flops 1815478272 | bytes 17104896 | tf_op jit(solution)/shard_map/ceik,kj->ceij/dot_general | solution.py:18
  184.9 5.7 %fusion.14 = f32[384,2,4,384]{0,3,2,1:T(8,128)} fusion(bf16[2,4,1,384,384]{4,3,1,0,2:T(8,128)(2,1)} %collective-permute-done.2, bf16[1,384,384]{1,2,0:T(8,128)(2,1)S(1)} %get-tuple-element.24), kind=kOutput, calls=%fused_computation.21 | convolution fusion | flops 905969664 | bytes 7372800 | tf_op jit(solution)/shard_map/ik,cekj->ceij/dot_general | solution.py:18
  190.5 7.9 %fusion.7 = f32[2,4,384,384]{3,2,1,0:T(8,128)} fusion(f32[384,2,4,384]{0,3,2,1:T(8,128)} %fusion.14, bf16[2,4,1,384,384]{4,3,2,1,0:T(8,128)(2,1)S(1)} %copy-done, bf16[1,384,384]{2,1,0:T(8,128)(2,1)} %collective-permute-done.3, bf16[1,384,384]{2,1,0:T(8,128)(2,1)S(1)} %copy-done.2), kind=kOutput, calls=%fused_computation.14 | convolution fusion | flops 1814298624 | bytes 12386304 | tf_op jit(solution)/shard_map/ceik,kj->ceij/dot_general | solution.py:18
  198.5 9.6 %add_add_fusion = f32[2,4,384,384]{3,2,1,0:T(8,128)} fusion(f32[2,4,384,384]{3,2,1,0:T(8,128)} %fusion.5, f32[2,4,384,384]{3,2,1,0:T(8,128)} %fusion.7, bf16[2,4,1,384,384]{4,3,1,0,2:T(8,128)(2,1)} %collective-permute-done.4, bf16[1,384,384]{1,2,0:T(8,128)(2,1)} %collective-permute-done.5, bf16[1,384,384]{1,2,0:T(8,128)(2,1)S(1)} %get-tuple-element.24), kind=kOutput, calls=%fused_computation.9 | convolution fusion | flops 1815478272 | bytes 17104896 | tf_op jit(solution)/shard_map/ceik,jk->ceij/dot_general | solution.py:18
  208.1 3.2 fusion.9
  211.3 2.6 convert_element_type.72
  214.0 2.7 reshape.315
  216.6 3.5 %copy.98 = bf16[2,4,48,3072]{3,1,2,0:T(4,128)(2,1)S(1)} copy(bf16[2,4,48,3072]{3,2,1,0:T(8,128)(2,1)} %reshape.315) | data formatting | bytes 4718592 | tf_op jit(solution)/shard_map/reshape | solution.py:120
  220.1 3.0 gather_fusion.2
  223.1 7.3 %fusion.42 = (bf16[2,4,4,8,3072]{4,2,1,0,3:T(4,128)(2,1)S(1)}, bf16[2,4,4,8,3072]{4,2,1,0,3:T(4,128)(2,1)}) fusion(bf16[4,8,2,4,3072]{4,3,2,1,0:T(4,128)(2,1)} %bitcast.167, pred[4,8]{0,1:T(8,128)(4,1)S(1)} %copy-done.4, bf16[4,8,2,4,3072]{4,3,2,1,0:T(4,128)(2,1)} %bitcast.168), kind=kLoop, calls=%fused_computation.37 | loop fusion | flops 1572864 | bytes 6291488 | tf_op jit(solution)/shard_map/jit(_take)/select_n | solution.py:121
  230.4 24.5 %all_to_all.45 = bf16[2,4,4,8,3072]{4,2,1,0,3:T(4,128)(2,1)S(1)} all-to-all(bf16[2,4,4,8,3072]{4,2,1,0,3:T(4,128)(2,1)S(1)} %get-tuple-element.27), channel_id=1, replica_groups=mesh['energy'=8,'space'=4] {'energy'}, dimensions={3} | all-to-all | bytes 3145728 | tf_op jit(solution)/shard_map/all_to_all | solution.py:127
  254.9 3.6 %all-to-all-start.1 = ((bf16[2,4,4,8,3072]{4,2,1,0,3:T(4,128)(2,1)}), bf16[2,4,4,8,3072]{4,2,1,0,3:T(4,128)(2,1)S(1)}, u32[]{:S(2)}, u32[]{:S(2)}) async-start(bf16[2,4,4,8,3072]{4,2,1,0,3:T(4,128)(2,1)} %get-tuple-element.28), calls=%async_computation.1 | async-start | bytes 3145728 | tf_op jit(solution)/shard_map/all_to_all | solution.py:128
  260.2 19.3 %all-to-all-done.1 = bf16[2,4,4,8,3072]{4,2,1,0,3:T(4,128)(2,1)S(1)} async-done(((bf16[2,4,4,8,3072]{4,2,1,0,3:T(4,128)(2,1)}), bf16[2,4,4,8,3072]{4,2,1,0,3:T(4,128)(2,1)S(1)}, u32[]{:S(2)}, u32[]{:S(2)}) %all-to-all-start.1) | async-done | bytes 1572896 | tf_op jit(solution)/shard_map/all_to_all | solution.py:128
  283.0 1.2 convert_element_type.74
  284.2 2.0 copy.101
  286.2 4.0 %all-to-all-start.2 = ((bf16[2,32,4,1,3072]{4,2,0,3,1:T(4,128)(2,1)}), bf16[2,32,4,1,3072]{4,2,0,3,1:T(4,128)(2,1)S(1)}, u32[]{:S(2)}, u32[]{:S(2)}) async-start(bf16[2,32,4,1,3072]{4,2,0,3,1:T(4,128)(2,1)} %copy.101), calls=%async_computation.2 | async-start | bytes 3145728 | tf_op jit(solution)/shard_map/all_to_all | solution.py:80
  290.6 20.6 %all-to-all-done.2 = bf16[2,32,4,1,3072]{4,2,0,3,1:T(4,128)(2,1)S(1)} async-done(((bf16[2,32,4,1,3072]{4,2,0,3,1:T(4,128)(2,1)}), bf16[2,32,4,1,3072]{4,2,0,3,1:T(4,128)(2,1)S(1)}, u32[]{:S(2)}, u32[]{:S(2)}) %all-to-all-start.2) | async-done | bytes 1572896 | tf_op jit(solution)/shard_map/all_to_all | solution.py:80
  312.6 1.2 copy.105
  313.8 4.1 %gather_fusion = bf16[48,2,4,3072]{3,2,1,0:T(4,128)(2,1)} fusion(bf16[2,4,32,3072]{3,1,2,0:T(4,128)(2,1)S(1)} %copy.105, s32[1024]{0:T(1024)S(1)} %pad_clamp_fusion), kind=kCustom, calls=%fused_computation.2 | custom fusion | bytes 4718784 | tf_op jit(solution)/shard_map/jit(_take)/gather | solution.py:133
  317.9 4.4 %copy.106 = bf16[2,4,48,3072]{3,2,1,0:T(8,128)(2,1)} copy(bf16[2,4,48,3072]{3,1,0,2:T(4,128)(2,1)} %bitcast.158) | data formatting | bytes 4718592 | tf_op jit(solution)/shard_map/jit(_take)/gather | solution.py:133
  322.3 3.7 %gather.10 = bf16[2,4,1,384,384]{4,3,1,0,2:T(8,128)(2,1)S(1)} reshape(bf16[2,4,48,3072]{3,2,1,0:T(8,128)(2,1)} %copy.106) | data formatting | bytes 4718592 | tf_op jit(solution)/shard_map/jit(_take)/gather | solution.py:133
  325.9 1.9 select_bitcast_fusion
  (54 shorter events, 12.0 us)
Async XLA Ops:
  0.0 175.4 %collective-permute-start.1 = (bf16[2,4,1,384,384]{4,3,1,0,2:T(8,128)(2,1)}, bf16[2,4,1,384,384]{4,3,1,0,2:T(8,128)(2,1)}, u32[]{:S(2)}, u32[]{:S(2)}) collective-permute-start(bf16[2,4,1,384,384]{4,3,1,0,2:T(8,128)(2,1)} %bitcast.156), channel_id=1, source_target_pairs={{0,1},{1,2},{2,3},{3,0},{4,5},{5,6},{6,7},{7,4},{8,9},{9,10},{10,1... | collective-permute-start | bytes 7077896 | tf_op jit(solution)/shard_map/ppermute | solution.py:14
  3.0 195.5 %collective-permute-start.4 = (bf16[2,4,1,384,384]{4,3,1,0,2:T(8,128)(2,1)}, bf16[2,4,1,384,384]{4,3,1,0,2:T(8,128)(2,1)}, u32[]{:S(2)}, u32[]{:S(2)}) collective-permute-start(bf16[2,4,1,384,384]{4,3,1,0,2:T(8,128)(2,1)} %bitcast.157), channel_id=1, source_target_pairs={{0,3},{1,0},{2,1},{3,2},{4,7},{5,4},{6,5},{7,6},{8,11},{9,8},{10,9... | collective-permute-start | bytes 7077896 | tf_op jit(solution)/shard_map/ppermute | solution.py:14
  7.0 107.4 %collective-permute-start = (bf16[1,384,384]{1,2,0:T(8,128)(2,1)S(1)}, bf16[1,384,384]{1,2,0:T(8,128)(2,1)}, u32[]{:S(2)}, u32[]{:S(2)}) collective-permute-start(bf16[1,384,384]{1,2,0:T(8,128)(2,1)S(1)} %get-tuple-element.24), channel_id=1, source_target_pairs={{0,1},{1,2},{2,3},{3,0},{4,5},{5,6},{6,7},{7,4},{8,9},{9,10},{10,1... | collective-permute-start | bytes 884744 | tf_op jit(solution)/shard_map/ppermute | solution.py:14
  7.0 177.9 %collective-permute-start.2 = (bf16[2,4,1,384,384]{4,3,1,0,2:T(8,128)(2,1)}, bf16[2,4,1,384,384]{4,3,1,0,2:T(8,128)(2,1)}, u32[]{:S(2)}, u32[]{:S(2)}) collective-permute-start(bf16[2,4,1,384,384]{4,3,1,0,2:T(8,128)(2,1)} %bitcast.169), channel_id=1, source_target_pairs={{0,3},{1,0},{2,1},{3,2},{4,7},{5,4},{6,5},{7,6},{8,11},{9,8},{10,9... | collective-permute-start | bytes 7077896 | tf_op jit(solution)/shard_map/ppermute | solution.py:14
  10.8 179.7 %collective-permute-start.3 = (bf16[1,384,384]{2,1,0:T(8,128)(2,1)}, bf16[1,384,384]{2,1,0:T(8,128)(2,1)}, u32[]{:S(2)}, u32[]{:S(2)}) collective-permute-start(bf16[1,384,384]{2,1,0:T(8,128)(2,1)} %param.14), channel_id=1, source_target_pairs={{0,3},{1,0},{2,1},{3,2},{4,7},{5,4},{6,5},{7,6},{8,11},{9,8},{10,9... | collective-permute-start | bytes 884744 | tf_op jit(solution)/shard_map/ppermute | solution.py:14
  26.2 5.5 %copy-start.1 = (bf16[2,4,1,384,384]{4,3,2,1,0:T(8,128)(2,1)S(1)}, bf16[2,4,1,384,384]{4,3,2,1,0:T(8,128)(2,1)}, u32[]{:S(2)}) copy-start(bf16[2,4,1,384,384]{4,3,2,1,0:T(8,128)(2,1)} %param.12) | copy-start | bytes 7077892
  26.2 5.5 %copy-start.2 = (bf16[1,384,384]{2,1,0:T(8,128)(2,1)S(1)}, bf16[1,384,384]{2,1,0:T(8,128)(2,1)}, u32[]{:S(2)}) copy-start(bf16[1,384,384]{2,1,0:T(8,128)(2,1)} %param.14) | copy-start | bytes 884740
  114.4 84.1 %collective-permute-start.5 = (bf16[1,384,384]{1,2,0:T(8,128)(2,1)S(1)}, bf16[1,384,384]{1,2,0:T(8,128)(2,1)}, u32[]{:S(2)}, u32[]{:S(2)}) collective-permute-start(bf16[1,384,384]{1,2,0:T(8,128)(2,1)S(1)} %get-tuple-element.24), channel_id=1, source_target_pairs={{0,3},{1,0},{2,1},{3,2},{4,7},{5,4},{6,5},{7,6},{8,11},{9,8},{10,9... | collective-permute-start | bytes 884744 | tf_op jit(solution)/shard_map/ppermute | solution.py:14
  184.9 5.7 %copy-start = (bf16[2,4,1,384,384]{4,3,2,1,0:T(8,128)(2,1)S(1)}, bf16[2,4,1,384,384]{4,3,2,1,0:T(8,128)(2,1)}, u32[]{:S(2)}) copy-start(bf16[2,4,1,384,384]{4,3,2,1,0:T(8,128)(2,1)} %param.13) | copy-start | bytes 7077892
  220.1 3.0 copy-start.4
  254.9 24.5 %all-to-all-start.1 = ((bf16[2,4,4,8,3072]{4,2,1,0,3:T(4,128)(2,1)}), bf16[2,4,4,8,3072]{4,2,1,0,3:T(4,128)(2,1)S(1)}, u32[]{:S(2)}, u32[]{:S(2)}) async-start(bf16[2,4,4,8,3072]{4,2,1,0,3:T(4,128)(2,1)} %get-tuple-element.28), calls=%async_computation.1 | async-start | bytes 3145728 | tf_op jit(solution)/shard_map/all_to_all | solution.py:128
  286.2 4.0 %copy-start.3 = (pred[48]{0:T(512)(128)(4,1)S(1)}, pred[48]{0:T(512)(128)(4,1)}, u32[]{:S(2)}) copy-start(pred[48]{0:T(512)(128)(4,1)} %get-tuple-element.20) | copy-start | bytes 148
  286.2 24.9 %all-to-all-start.2 = ((bf16[2,32,4,1,3072]{4,2,0,3,1:T(4,128)(2,1)}), bf16[2,32,4,1,3072]{4,2,0,3,1:T(4,128)(2,1)S(1)}, u32[]{:S(2)}, u32[]{:S(2)}) async-start(bf16[2,32,4,1,3072]{4,2,0,3,1:T(4,128)(2,1)} %copy.101), calls=%async_computation.2 | async-start | bytes 3145728 | tf_op jit(solution)/shard_map/all_to_all | solution.py:80
where the time goes:
time: 334 us; the launch traced here: 328 us
  waiting for transfers between devices  119 us (36%)
  starting transfers between devices  77.7 us (23%)
  local copies, waits for them, and re-layouts  44.1 us (13%)
  matrix products  43.4 us (13%)
  blocking collectives  24.5 us (7%)
  other arithmetic  18.2 us (5%)
    ppermute x6, waiting for transfers between devices, shifted(): return lax.ppermute(value, axis, pairs)  79.2 us
    ppermute x6, starting transfers between devices, shifted(): return lax.ppermute(value, axis, pairs)  70.2 us
    dot_general x6, matrix products, product(): return jnp.einsum(form, left, right, preferred_element_type=jnp.float32)  41.5 us
    all_to_all x1, blocking collectives, per_device(): lax.all_to_all(send_green, 'energy', split_axis=3, concat_axis=1, tiled=T...  24.5 us
    all_to_all x1, waiting for transfers between devices, convolve(): lax.all_to_all(result, 'energy', split_axis=1, concat_axis=3, tiled=True)  20.6 us
    all_to_all x1, waiting for transfers between devices, per_device(): lax.all_to_all(send_screen, 'energy', split_axis=3, concat_axis=1, tiled=...  19.3 us
    gather x3, local copies, waits for them, and re-layouts, per_device(): chosen = jnp.take(returned, picking, axis=2)  12.2 us
    gather x2, local copies, waits for them, and re-layouts, arrange(): return jnp.take(grouped, source_group.T, axis=2)  7.72 us
  transfers between devices with their start and end apart: 8, of which 3 were waited for; matrix products, arithmetic and copies ran while one was open for 15% of the time, Pallas kernels for 0%

commit v1 on v0

v1 whole, which is shorter than its diff:
```python
import math

import jax
import jax.numpy as jnp
from jax import lax
from jax.sharding import PartitionSpec as P

LIVE = 30
BF = jnp.bfloat16
F32 = jnp.float32


def shifted(value, axis, steps):
    count = lax.axis_size(axis)
    pairs = [(source, (source + steps) % count) for source in range(count)]
    return lax.ppermute(value, axis, pairs)


def product(form, left, right):
    return jnp.einsum(form, left, right, preferred_element_type=F32)


def transform_tables(energies, peers):
    local = energies // peers
    ids = jnp.arange(2 * energies, dtype=jnp.int32)
    part = ids // local % 2
    energy = ids // (2 * local) * local + ids % local
    phases = energy[:, None] * energy[None, :] % energies
    angles = 2.0 * math.pi / energies * phases.astype(F32)
    cosine = jnp.cos(angles)
    sine = jnp.sin(angles)
    out_im = part[:, None] == 1
    in_im = part[None, :] == 1
    forward = jnp.where(out_im == in_im, cosine, jnp.where(in_im, sine, -sine))
    inverse = jnp.where(out_im == in_im, -sine, jnp.where(in_im, -cosine, cosine))
    return forward.astype(BF), (inverse / (energies * math.sqrt(energies))).astype(BF)


def selection(present_row, orbitals, rows):
    width = orbitals // present_row.shape[0]
    live = jnp.repeat(present_row, width) > 0
    ids = jnp.arange(orbitals, dtype=jnp.int32)
    before = (ids[:, None] < ids[None, :]) & live[:, None]
    rank = jnp.sum(before.astype(jnp.int32), axis=0)
    return (live[None, :] & (rank[None, :] == jnp.arange(rows, dtype=jnp.int32)[:, None])).astype(BF)


def per_device(g_upper, p_diag, p_upper, v_diag, v_upper, v_pattern, element_present):
    peers = lax.axis_size("energy")
    local = p_diag.shape[1]
    orbitals = p_diag.shape[3]
    groups = element_present.shape[1]
    slots = (LIVE + peers - 1) // peers
    share = slots * (orbitals // groups)
    rows = peers * share
    batch = 2 * local
    energies = local * peers

    def flat(value):
        return value.reshape(batch, orbitals, orbitals)

    g, pd, pu = flat(g_upper), flat(p_diag), flat(p_upper)
    vd = v_diag[0]
    vu = v_upper[0] * v_pattern.astype(BF)[:, None]
    pick = selection(element_present[0], orbitals, rows)
    own_vu = product("rk,kj->rj", pick, vu).astype(BF)
    prev_vu = shifted(own_vu, "space", 1)
    present_next = shifted(element_present, "space", -1)
    vd_next = shifted(vd, "space", -1)
    own_vd = product("rk,kj->rj", pick, vd).astype(BF)
    pick_next = selection(present_next[0], orbitals, rows)
    next_vu = product("rk,jk->rj", pick_next, vu).astype(BF)
    left = product("rk,bkj->brj", next_vu, pu).astype(BF)
    left_in = shifted(left, "space", 1)
    right = product(
        "brk,kj->brj", product("rk,bkj->brj", prev_vu, pd).astype(BF), vd
    ) + product("brk,jk->brj", product("rk,bkj->brj", prev_vu, pu).astype(BF), vu)
    right_in = shifted(right.astype(BF), "space", -1)

    def spread(value):
        return lax.all_to_all(value, "energy", split_axis=0, concat_axis=0, tiled=True)

    send_green = jnp.moveaxis(
        product("rk,bkj->brj", pick, g).astype(BF).reshape(batch, peers, share, orbitals), 1, 0
    )
    green = spread(send_green)
    same = product("rk,bkj->brj", own_vd, pd) + product("rk,bjk->brj", own_vu, pu)
    one = product("rk,bkj->brj", own_vd, pu).astype(BF)
    total = product("brk,kj->brj", one, vd_next)
    real = (jnp.arange(batch, dtype=jnp.int32) < local).astype(F32)
    total = total + real[:, None, None] * own_vu.astype(F32)
    total = total + right_in.astype(F32)
    total = total + product("brk,kj->brj", (same + left_in.astype(F32)).astype(BF), vu)
    send_screen = jnp.moveaxis(total.astype(BF).reshape(batch, peers, share, orbitals), 1, 0)
    screen = spread(send_screen)

    forward, inverse = transform_tables(energies, peers)
    columns = share * orbitals

    def spectrum(values):
        freq = jnp.dot(forward, values.reshape(2 * energies, columns), preferred_element_type=F32)
        return freq.reshape(peers, 2, local, columns)

    green_freq = spectrum(green)
    screen_freq = spectrum(screen)
    g_re, g_im = green_freq[:, 0], green_freq[:, 1]
    s_re, s_im = screen_freq[:, 0], screen_freq[:, 1]
    mixed = jnp.stack([g_re * s_re - g_im * s_im, g_re * s_im + g_im * s_re], 1)
    mixed = mixed.reshape(2 * energies, columns).astype(BF)
    sigma = jnp.dot(inverse, mixed, preferred_element_type=F32).astype(BF)
    back = spread(sigma.reshape(peers, batch, share, orbitals))
    back = jnp.moveaxis(back, 0, 1).reshape(batch, rows, orbitals)
    out = product("rk,brj->bkj", pick, back).astype(BF)
    return out.reshape(2, local, 1, orbitals, orbitals)


def solution(mesh):
    in_specs = (
        P(None, "energy", "space", None, None),
        P(None, "energy", "space", None, None),
        P(None, "energy", "space", None, None),
        P("space", None, None),
        P("space", None, None),
        P("space"),
        P("space", None),
    )
    out_specs = P(None, "energy", "space", None, None)
    return jax.shard_map(
        per_device, mesh=mesh, in_specs=in_specs, out_specs=out_specs, check_vma=False
    )
```

time: 334 us -> 172 us (0.51)
  starting transfers between devices: 77.7 us -> 15.2 us
  waiting for transfers between devices: 119 us -> 60.3 us
  local copies, waits for them, and re-layouts: 44.1 us -> 22.5 us
  other arithmetic: 18.2 us -> 1.54 us
    ppermute x6 -> x5, starting transfers between devices: 70.2 us -> 6.36 us  [shifted(): return lax.ppermute(value, axis, pairs)]
    ppermute x6 -> x5, waiting for transfers between devices: 79.2 us -> 46.9 us  [shifted(): return lax.ppermute(value, axis, pairs)]
    all_to_all x2, waiting for transfers between devices: 39.9 us -> 13.4 us  [spread(): lax.all_to_all(value, 'energy', split_axis=0, concat_axis=0, tiled=True)]
    gather x5 -> x0, local copies, waits for them, and re-layouts: 19.9 us -> none  [the longest x3 12.2 us: per_device(): chosen = jnp.take(returned, picking, axis=2)]
    select_n x4 -> x0, other arithmetic: 9.37 us -> none  [the longest x2 7.34 us: arrange(): return jnp.take(grouped, source_group.T, axis=2)]
    reshape x3 -> x6, local copies, waits for them, and re-layouts: 7.39 us -> 15.9 us  [the longest x2 7.14 us: spectrum(): values.reshape(2 * energies, columns)]
    another operation x2 -> x1, local copies, waits for them, and re-layouts: 6.9 us -> 2.36 us  [per_device(): mixed = jnp.stack([g_re * s_re - g_im * s_im, g_re * s_im + g_im * s_re], 1)]
    dot_general x9 -> x13, matrix products: 43.4 us -> 44.8 us  [the longest x10 36.5 us: product(): return jnp.einsum(form, left, right, preferred_element_type=F32)]
  transfers between devices with their start and end apart: 8 -> 7, of which waited for: 3 -> 4; matrix products, arithmetic and copies ran while one was open for 15% -> 28% of each run, Pallas kernels for 0% -> 0%
where the time goes in v1:
time: 172 us; the launch traced here: 168 us
  waiting for transfers between devices  60.3 us (35%)
  matrix products  44.8 us (26%)
  blocking collectives  23.4 us (14%)
  local copies, waits for them, and re-layouts  22.5 us (13%)
  starting transfers between devices  15.2 us (9%)
    ppermute x5, waiting for transfers between devices, shifted(): return lax.ppermute(value, axis, pairs)  46.9 us
    dot_general x10, matrix products, product(): return jnp.einsum(form, left, right, preferred_element_type=F32)  36.5 us
    all_to_all x1, blocking collectives, spread(): lax.all_to_all(value, 'energy', split_axis=0, concat_axis=0, tiled=True)  23.4 us
    all_to_all x2, waiting for transfers between devices, spread(): lax.all_to_all(value, 'energy', split_axis=0, concat_axis=0, tiled=True)  13.4 us
    all_to_all x2, starting transfers between devices, spread(): lax.all_to_all(value, 'energy', split_axis=0, concat_axis=0, tiled=True)  8.79 us
    reshape x2, local copies, waits for them, and re-layouts, spectrum(): values.reshape(2 * energies, columns)  7.14 us
    ppermute x5, starting transfers between devices, shifted(): return lax.ppermute(value, axis, pairs)  6.36 us
    dot_general x2, matrix products, spectrum(): jnp.dot(forward, values.reshape(2 * energies, columns), preferred_element...  6.12 us
  transfers between devices with their start and end apart: 7, of which 4 were waited for; matrix products, arithmetic and copies ran while one was open for 28% of the time, Pallas kernels for 0%

profile of v1, /device:TPU:0, one launch (start us, length us, event | category | flops | bytes accessed | tf_op | source)
XLA Modules:
  0.0 168.5 jit_solution(6158855396681270670)
XLA Ops:
  0.0 5.0 %collective-permute-start.3 = (s32[1,48]{1,0:T(1,128)}, s32[1,48]{1,0:T(1,128)S(1)}, u32[]{:S(2)}, u32[]{:S(2)}) collective-permute-start(s32[1,48]{1,0:T(1,128)} %param.13), channel_id=1, source_target_pairs={{0,3},{1,0},{2,1},{3,2},{4,7},{5,4},{6,5},{7,6},{8,11},{9,8},{10,9... | collective-permute-start | bytes 584 | tf_op jit(solution)/shard_map/ppermute | solution.py:16
  5.1 0.7 compare_bitcast_fusion.1
  6.7 1.3 fusion.110
  8.4 3.3 %fusion.12 = bf16[8,256,384]{2,1,0:T(8,128)(2,1)} fusion(bf16[8,384,384]{2,1,0:T(8,128)(2,1)S(1)} %bitcast.111, s32[384]{0:T(512)S(1)} %convert_reduce_fusion, pred[384]{0:T(512)(128)(4,1)S(1)} %gt.41, bf16[1,384,384]{2,1,0:T(8,128)(2,1)} %param.11, bf16[]{:T(256)} %bitcast.12), kind=kOutput, calls=%fused_computation.25 | convolution fusion | flops 680706048 | bytes 4228994 | tf_op jit(solution)/shard_map/rk,bkj->brj/dot_general | solution.py:20
  11.9 4.6 %collective-permute-done.1 = bf16[256,384]{1,0:T(8,128)(2,1)S(1)} collective-permute-done((bf16[256,384]{1,0:T(8,128)(2,1)S(1)}, bf16[256,384]{1,0:T(8,128)(2,1)S(1)}, u32[]{:S(2)}, u32[]{:S(2)}) %collective-permute-start.1) | collective-permute-done | bytes 196640 | tf_op jit(solution)/shard_map/ppermute | solution.py:16
  16.5 5.3 %fusion.4 = f32[8,256,384]{2,1,0:T(8,128)} fusion(bf16[8,384,384]{2,1,0:T(8,128)(2,1)} %bitcast.113, bf16[1,384,384]{2,1,0:T(8,128)(2,1)} %param.10, bf16[256,384]{1,0:T(8,128)(2,1)S(1)} %collective-permute-done.1), kind=kOutput, calls=%fused_computation.15 | convolution fusion | flops 1208745984 | bytes 5996544 | tf_op jit(solution)/shard_map/brk,kj->brj/dot_general | solution.py:20
  21.8 5.0 %add_convert_fusion.1 = bf16[8,256,384]{2,1,0:T(8,128)(2,1)} fusion(f32[8,256,384]{2,1,0:T(8,128)} %fusion.4, bf16[8,384,384]{2,1,0:T(8,128)(2,1)S(1)} %bitcast.109, bf16[256,384]{1,0:T(8,128)(2,1)S(1)} %collective-permute-done.1, bf16[1,384,384]{2,1,0:T(8,128)(2,1)S(1)} %copy-done.2, bf16[]{:T(256)} %bitcast.12), kind=kOutput, calls=%fused_computation.4 | convolution fusion | flops 1210466304 | bytes 7569410 | tf_op jit(solution)/shard_map/brk,jk->brj/dot_general | solution.py:20
  26.8 1.1 collective-permute-start
  27.9 2.6 %convolution_convert_fusion.6 = bf16[256,8,384]{2,0,1:T(8,128)(2,1)S(1)} fusion(bf16[8,384,384]{2,1,0:T(8,128)(2,1)} %bitcast.120, s32[384]{0:T(512)S(1)} %convert_reduce_fusion.1, pred[384]{0:T(512)(128)(4,1)S(1)} %gt.38), kind=kOutput, calls=%fused_computation.10 | convolution fusion | flops 604962816 | bytes 3934080 | tf_op jit(solution)/shard_map/rk,bkj->brj/dot_general | solution.py:20
  30.5 1.4 copy.38
  31.9 4.3 %all-to-all-start = ((bf16[8,8,32,384]{3,2,1,0:T(8,128)(2,1)}), bf16[8,8,32,384]{3,2,1,0:T(8,128)(2,1)}, u32[]{:S(2)}, u32[]{:S(2)}) async-start(bf16[8,8,32,384]{3,2,1,0:T(8,128)(2,1)} %bitcast.115), calls=%async_computation | async-start | bytes 3145728 | tf_op jit(solution)/shard_map/all_to_all | solution.py:81
  36.2 1.3 fusion.14
  37.5 4.3 %fusion.111 = f32[256,8,384]{2,0,1:T(8,128)} fusion(bf16[256,384,1]{1,0,2:T(8,128)(2,1)S(1)} %fusion.14, bf16[8,384,384]{2,1,0:T(8,128)(2,1)} %bitcast.114), kind=kOutput, calls=%fused_computation.150 | convolution fusion | flops 603979776 | bytes 5701632 | tf_op jit(solution)/shard_map/rk,bkj->brj/dot_general | solution.py:20
  41.9 9.4 %collective-permute-done.4 = bf16[8,256,384]{2,1,0:T(8,128)(2,1)} collective-permute-done((bf16[8,256,384]{2,1,0:T(8,128)(2,1)}, bf16[8,256,384]{2,1,0:T(8,128)(2,1)}, u32[]{:S(2)}, u32[]{:S(2)}) %collective-permute-start.4) | collective-permute-done | bytes 1572896 | tf_op jit(solution)/shard_map/ppermute | solution.py:16
  51.3 6.0 %fusion.13 = f32[8,256,384]{2,1,0:T(8,128)} fusion(bf16[8,256,384]{2,1,0:T(8,128)(2,1)} %collective-permute-done.4, f32[256,8,384]{2,0,1:T(8,128)} %fusion.111, bf16[8,384,384]{2,1,0:T(8,128)(2,1)S(1)} %bitcast.110, bf16[256,384]{1,0:T(8,128)(2,1)S(1)} %get-tuple-element.8, bf16[1,384,384]{2,1,0:T(8,128)(2,1)S(1)} %copy-done.2, bf16[]{:T(256)} %bitcast.12), kind=kOutput, calls=%fused_computation.26 | convolution fusion | flops 1211252736 | bytes 10715138 | tf_op jit(solution)/shard_map/brk,kj->brj/dot_general | solution.py:20
  57.3 32.9 %collective-permute-done = bf16[384,384]{1,0:T(8,128)(2,1)} collective-permute-done((bf16[384,384]{1,0:T(8,128)(2,1)}, bf16[384,384]{1,0:T(8,128)(2,1)}, u32[]{:S(2)}, u32[]{:S(2)}) %collective-permute-start) | collective-permute-done | bytes 294944 | tf_op jit(solution)/shard_map/ppermute | solution.py:16
  90.2 4.9 %add_convert_fusion = bf16[8,256,384]{2,1,0:T(8,128)(2,1)} fusion(f32[8,256,384]{2,1,0:T(8,128)} %fusion.13, bf16[8,256,384]{2,1,0:T(8,128)(2,1)} %collective-permute-done.2, f32[256,384]{1,0:T(8,128)S(1)} %get-tuple-element.7, f32[8]{0:T(128)S(1)} %compare_convert_fusion, bf16[256,384,1]{1,0,2:T(8,128)(2,1)S(1)} %fusion.14, ...), kind=kOutput, calls=%fused_computation.3 | convolution fusion | flops 1213464576 | bytes 9535520 | tf_op jit(solution)/shard_map/brk,kj->brj/dot_general | solution.py:20
  95.1 2.8 %copy.37 = bf16[8,8,32,384]{3,2,0,1:T(8,128)(2,1)} copy(bf16[8,8,32,384]{3,2,1,0:T(8,128)(2,1)} %bitcast.121) | data formatting | bytes 3145728 | tf_op jit(solution)/shard_map/reshape | solution.py:94
  97.9 4.5 %all-to-all-start.1 = ((bf16[8,8,32,384]{3,2,1,0:T(8,128)(2,1)}), bf16[8,8,32,384]{3,2,1,0:T(8,128)(2,1)}, u32[]{:S(2)}, u32[]{:S(2)}) async-start(bf16[8,8,32,384]{3,2,1,0:T(8,128)(2,1)} %bitcast.116), calls=%async_computation.1 | async-start | bytes 3145728 | tf_op jit(solution)/shard_map/all_to_all | solution.py:81
  102.5 3.6 %reshape.264 = bf16[64,12288,1,1]{1,0,2,3:T(8,128)(2,1)} reshape(bf16[8,8,32,384]{3,2,1,0:T(8,128)(2,1)} %all-to-all-done) | data formatting | bytes 3145728 | tf_op jit(solution)/shard_map/reshape | solution.py:101
  106.0 3.8 %fusion.10 = f32[8,2,4,12288]{3,0,2,1:T(8,128)} fusion(bf16[64,12288,1,1]{1,0,2,3:T(8,128)(2,1)} %reshape.264, s32[64]{0:T(128)S(1)} %fusion.92, s32[8,2,4]{0,2,1:T(4,128)S(1)} %fusion.88, pred[64]{0:T(512)(128)(4,1)S(1)} %fusion.94, pred[8,2,4]{0,2,1:T(4,128)(4,1)S(1)} %fusion.86), kind=kOutput, calls=%fused_computation.19 | convolution fusion | flops 100741120 | bytes 4719232 | tf_op jit(solution)/shard_map/dot_general | solution.py:101
  109.8 13.4 %all-to-all-done.1 = bf16[8,8,32,384]{3,2,1,0:T(8,128)(2,1)} async-done(((bf16[8,8,32,384]{3,2,1,0:T(8,128)(2,1)}), bf16[8,8,32,384]{3,2,1,0:T(8,128)(2,1)}, u32[]{:S(2)}, u32[]{:S(2)}) %all-to-all-start.1) | async-done | bytes 1572896 | tf_op jit(solution)/shard_map/all_to_all | solution.py:81
  123.2 3.6 %reshape.272 = bf16[64,12288,1,1]{1,0,2,3:T(8,128)(2,1)} reshape(bf16[8,8,32,384]{3,2,1,0:T(8,128)(2,1)} %all-to-all-done.1) | data formatting | bytes 3145728 | tf_op jit(solution)/shard_map/reshape | solution.py:101
  126.8 2.3 %fusion.1 = f32[8,2,4,12288]{3,0,2,1:T(8,128)S(1)} fusion(bf16[64,12288,1,1]{1,0,2,3:T(8,128)(2,1)} %reshape.272, s32[64]{0:T(128)S(1)} %fusion.92, s32[8,2,4]{0,2,1:T(4,128)S(1)} %fusion.88, pred[64]{0:T(512)(128)(4,1)S(1)} %fusion.94, pred[8,2,4]{0,2,1:T(4,128)(4,1)S(1)} %fusion.86), kind=kOutput, calls=%fused_computation.12 | convolution fusion | flops 100741120 | bytes 4719232 | tf_op jit(solution)/shard_map/dot_general | solution.py:101
  129.2 0.4 subtract_convert_fusion
  129.7 2.4 %copy.27 = bf16[8,2,4,12288]{3,2,1,0:T(4,128)(2,1)} copy(bf16[8,2,4,12288]{3,0,2,1:T(8,128)(2,1)S(1)} %pad_maximum_fusion) | data formatting | bytes 3145728 | tf_op jit(solution)/shard_map/stack | solution.py:108
  132.1 3.7 %convert_element_type.144 = bf16[64,12288]{1,0:T(8,128)(2,1)} reshape(bf16[8,2,4,12288]{3,2,1,0:T(4,128)(2,1)} %copy.27) | data formatting | bytes 3145728 | tf_op jit(solution)/shard_map/convert_element_type | solution.py:109
  135.7 2.2 %convolution_convert_fusion = bf16[64,12288]{1,0:T(8,128)(2,1)S(1)} fusion(bf16[64,12288]{1,0:T(8,128)(2,1)} %convert_element_type.144, s32[64]{0:T(128)S(1)} %fusion.92, pred[64]{0:T(512)(128)(4,1)S(1)} %fusion.94), kind=kOutput, calls=%fused_computation | convolution fusion | flops 101535744 | bytes 3146048 | tf_op jit(solution)/shard_map/dot_general | solution.py:110
  137.9 0.3 copy.28
  138.1 23.4 %all_to_all.15 = bf16[8,8,32,384]{3,2,1,0:T(8,128)(2,1)S(1)} all-to-all(bf16[8,8,32,384]{3,2,1,0:T(8,128)(2,1)S(1)} %copy.28), channel_id=1, replica_groups=mesh['energy'=8,'space'=4] {'energy'}, dimensions={0} | all-to-all | bytes 3145728 | tf_op jit(solution)/shard_map/all_to_all | solution.py:81
  161.8 2.5 %convolution_convert_fusion.1 = bf16[8,384,384]{2,1,0:T(8,128)(2,1)} fusion(bf16[8,256,384]{2,1,0:T(8,128)(2,1)S(1)} %bitcast.118, s32[384]{0:T(512)S(1)} %convert_reduce_fusion.1, pred[384]{0:T(512)(128)(4,1)S(1)} %gt.38), kind=kOutput, calls=%fused_computation.5 | convolution fusion | flops 605356032 | bytes 3934080 | tf_op jit(solution)/shard_map/rk,brj->bkj/dot_general | solution.py:20
  164.2 4.3 %copy.31 = bf16[2,4,1,384,384]{4,3,2,1,0:T(8,128)(2,1)} copy(bf16[2,4,1,384,384]{3,4,1,0,2:T(8,128)(2,1)} %bitcast.112) | data formatting | bytes 4718592 | tf_op jit(solution)/shard_map/reshape | solution.py:114
  (26 shorter events, 1.3 us)
Async XLA Ops:
  0.0 8.4 %copy-start = (bf16[2,4,1,384,384]{4,3,2,1,0:T(8,128)(2,1)S(1)}, bf16[2,4,1,384,384]{4,3,2,1,0:T(8,128)(2,1)}, u32[]{:S(2)}) copy-start(bf16[2,4,1,384,384]{4,3,2,1,0:T(8,128)(2,1)} %param.9) | copy-start | bytes 7077892
  0.0 8.1 %collective-permute-start.3 = (s32[1,48]{1,0:T(1,128)}, s32[1,48]{1,0:T(1,128)S(1)}, u32[]{:S(2)}, u32[]{:S(2)}) collective-permute-start(s32[1,48]{1,0:T(1,128)} %param.13), channel_id=1, source_target_pairs={{0,3},{1,0},{2,1},{3,2},{4,7},{5,4},{6,5},{7,6},{8,11},{9,8},{10,9... | collective-permute-start | bytes 584 | tf_op jit(solution)/shard_map/ppermute | solution.py:16
  8.0 8.5 %collective-permute-start.1 = (bf16[256,384]{1,0:T(8,128)(2,1)S(1)}, bf16[256,384]{1,0:T(8,128)(2,1)S(1)}, u32[]{:S(2)}, u32[]{:S(2)}) collective-permute-start(bf16[256,384]{1,0:T(8,128)(2,1)S(1)} %get-tuple-element.8), channel_id=1, source_target_pairs={{0,1},{1,2},{2,3},{3,0},{4,5},{5,6},{6,7},{7,4},{8,9},{9,10},{10,1... | collective-permute-start | bytes 589832 | tf_op jit(solution)/shard_map/ppermute | solution.py:16
  11.7 39.5 %collective-permute-start.4 = (bf16[8,256,384]{2,1,0:T(8,128)(2,1)}, bf16[8,256,384]{2,1,0:T(8,128)(2,1)}, u32[]{:S(2)}, u32[]{:S(2)}) collective-permute-start(bf16[8,256,384]{2,1,0:T(8,128)(2,1)} %fusion.12), channel_id=1, source_target_pairs={{0,1},{1,2},{2,3},{3,0},{4,5},{5,6},{6,7},{7,4},{8,9},{9,10},{10,1... | collective-permute-start | bytes 4718600 | tf_op jit(solution)/shard_map/ppermute | solution.py:16
  16.5 5.3 %copy-start.2 = (bf16[1,384,384]{2,1,0:T(8,128)(2,1)S(1)}, bf16[1,384,384]{2,1,0:T(8,128)(2,1)}, u32[]{:S(2)}) copy-start(bf16[1,384,384]{2,1,0:T(8,128)(2,1)} %param.11) | copy-start | bytes 884740
  26.8 63.4 %collective-permute-start.2 = (bf16[8,256,384]{2,1,0:T(8,128)(2,1)}, bf16[8,256,384]{2,1,0:T(8,128)(2,1)}, u32[]{:S(2)}, u32[]{:S(2)}) collective-permute-start(bf16[8,256,384]{2,1,0:T(8,128)(2,1)} %add_convert_fusion.1), channel_id=1, source_target_pairs={{0,3},{1,0},{2,1},{3,2},{4,7},{5,4},{6,5},{7,6},{8,11},{9,8},{10,9... | collective-permute-start | bytes 4718600 | tf_op jit(solution)/shard_map/ppermute | solution.py:16
  26.8 63.4 %collective-permute-start = (bf16[384,384]{1,0:T(8,128)(2,1)}, bf16[384,384]{1,0:T(8,128)(2,1)}, u32[]{:S(2)}, u32[]{:S(2)}) collective-permute-start(bf16[384,384]{1,0:T(8,128)(2,1)} %bitcast.122), channel_id=1, source_target_pairs={{0,3},{1,0},{2,1},{3,2},{4,7},{5,4},{6,5},{7,6},{8,11},{9,8},{10,9... | collective-permute-start | bytes 884744 | tf_op jit(solution)/shard_map/ppermute | solution.py:16
  31.9 65.9 %all-to-all-start = ((bf16[8,8,32,384]{3,2,1,0:T(8,128)(2,1)}), bf16[8,8,32,384]{3,2,1,0:T(8,128)(2,1)}, u32[]{:S(2)}, u32[]{:S(2)}) async-start(bf16[8,8,32,384]{3,2,1,0:T(8,128)(2,1)} %bitcast.115), calls=%async_computation | async-start | bytes 3145728 | tf_op jit(solution)/shard_map/all_to_all | solution.py:81
  97.9 25.4 %all-to-all-start.1 = ((bf16[8,8,32,384]{3,2,1,0:T(8,128)(2,1)}), bf16[8,8,32,384]{3,2,1,0:T(8,128)(2,1)}, u32[]{:S(2)}, u32[]{:S(2)}) async-start(bf16[8,8,32,384]{3,2,1,0:T(8,128)(2,1)} %bitcast.116), calls=%async_computation.1 | async-start | bytes 3145728 | tf_op jit(solution)/shard_map/all_to_all | solution.py:81
  126.8 2.4 %copy-start.1 = (f32[8,2,4,12288]{3,0,2,1:T(8,128)S(1)}, f32[8,2,4,12288]{3,0,2,1:T(8,128)}, u32[]{:S(2)}) copy-start(f32[8,2,4,12288]{3,0,2,1:T(8,128)} %fusion.10) | copy-start | bytes 9437188

commit v2 on v1

v2 whole, which is shorter than its diff:
```python
import math

import jax
import jax.numpy as jnp
import ml_dtypes
import numpy as np
from jax import lax
from jax.experimental import pallas as pl
from jax.experimental.pallas import tpu as pltpu
from jax.sharding import PartitionSpec as P

LIVE = 30
CHUNKS = 2
BF = jnp.bfloat16
F32 = jnp.float32


def shifted(value, axis, steps):
    count = lax.axis_size(axis)
    pairs = [(source, (source + steps) % count) for source in range(count)]
    return lax.ppermute(value, axis, pairs)


def product(form, left, right):
    return jnp.einsum(form, left, right, preferred_element_type=F32)


def transform_tables(energies, peers, share):
    local = energies // peers
    part_in = np.arange(2 * energies) // local % 2
    energy_in = np.arange(2 * energies) // (2 * local) * local + np.arange(2 * energies) % local
    part = np.arange(2 * energies) // energies
    energy = np.arange(2 * energies) % energies
    angles = 2.0 * math.pi / energies * (energy[:, None] * energy_in[None, :] % energies)
    cosine, sine = np.cos(angles), np.sin(angles)
    same = part[:, None] == part_in[None, :]
    forward = np.where(same, cosine, np.where(part_in[None, :] == 1, sine, -sine))
    inverse = np.where(same, -sine, np.where(part[:, None] == 1, -cosine, cosine)).T
    inverse = inverse / (energies * math.sqrt(energies))
    eye = np.eye(share)
    return (
        jnp.asarray(np.kron(forward, eye).astype(ml_dtypes.bfloat16)),
        jnp.asarray(np.kron(inverse, eye).astype(ml_dtypes.bfloat16)),
    )


def convolve_kernel(green_ref, screen_ref, forward_ref, inverse_ref, out_ref):
    half = forward_ref.shape[0] // 2
    green = jnp.dot(forward_ref[...], green_ref[...], preferred_element_type=F32)
    screen = jnp.dot(forward_ref[...], screen_ref[...], preferred_element_type=F32)
    g_re, g_im, s_re, s_im = green[:half], green[half:], screen[:half], screen[half:]
    real = (g_re * s_re - g_im * s_im).astype(BF)
    imag = (g_re * s_im + g_im * s_re).astype(BF)
    out_ref[...] = (
        jnp.dot(inverse_ref[:, :half], real, preferred_element_type=F32)
        + jnp.dot(inverse_ref[:, half:], imag, preferred_element_type=F32)
    ).astype(BF)


def convolve(green, screen, forward, inverse):
    count, columns = green.shape
    tile = 128 if columns % 128 == 0 else columns
    block = pl.BlockSpec((count, tile), lambda j: (0, j))
    table = pl.BlockSpec((count, count), lambda j: (0, 0))
    return pl.pallas_call(
        convolve_kernel,
        out_shape=jax.ShapeDtypeStruct((count, columns), BF),
        grid=(columns // tile,),
        in_specs=[block, block, table, table],
        out_specs=block,
        compiler_params=pltpu.CompilerParams(vmem_limit_bytes=48 << 20),
        cost_estimate=pl.CostEstimate(
            flops=6 * count * count * columns,
            bytes_accessed=4 * count * count + 6 * count * columns,
            transcendentals=0,
        ),
    )(green, screen, forward, inverse)


def selection(present_row, orbitals, rows):
    width = orbitals // present_row.shape[0]
    live = jnp.repeat(present_row, width) > 0
    ids = jnp.arange(orbitals, dtype=jnp.int32)
    before = (ids[:, None] < ids[None, :]) & live[:, None]
    rank = jnp.sum(before.astype(jnp.int32), axis=0)
    return (live[None, :] & (rank[None, :] == jnp.arange(rows, dtype=jnp.int32)[:, None])).astype(BF)


def per_device(g_upper, p_diag, p_upper, v_diag, v_upper, v_pattern, element_present):
    peers = lax.axis_size("energy")
    local = p_diag.shape[1]
    orbitals = p_diag.shape[3]
    width = orbitals // element_present.shape[1]
    slots = (LIVE + peers - 1) // peers
    chunks = CHUNKS if slots % CHUNKS == 0 else 1
    share = slots // chunks * width
    rows = peers * share
    batch = 2 * local
    energies = local * peers

    def flat(value):
        return value.reshape(batch, orbitals, orbitals)

    def spread(value):
        return lax.all_to_all(value, "energy", split_axis=0, concat_axis=0, tiled=True)

    def by_peer(value):
        return jnp.moveaxis(value.reshape(batch, peers, share, orbitals), 1, 0)

    g, pd, pu = flat(g_upper), flat(p_diag), flat(p_upper)
    vd = v_diag[0]
    vu = v_upper[0] * v_pattern.astype(BF)[:, None]
    pick = selection(element_present[0], orbitals, chunks * rows)
    own_vu = product("rk,kj->rj", pick, vu).astype(BF)
    prev_vu = shifted(own_vu[: LIVE * width], "space", 1)
    present_next = shifted(element_present, "space", -1)
    pick_next = selection(present_next[0], orbitals, LIVE * width)
    next_vu = product("rk,jk->rj", pick_next, vu).astype(BF)

    left_in, right_in, sent = [], [], []
    feed, prev_feed = next_vu, prev_vu
    for c in range(chunks):
        part = slice(c * rows, min((c + 1) * rows, LIVE * width))
        left = product("rk,bkj->brj", feed[part], pu).astype(BF)
        right = product(
            "brk,kj->brj", product("rk,bkj->brj", prev_feed[part], pd).astype(BF), vd
        ) + product("brk,jk->brj", product("rk,bkj->brj", prev_feed[part], pu).astype(BF), vu)
        right = right.astype(BF)
        left, right, feed, prev_feed, vd_last = lax.optimization_barrier(
            (left, right, feed, prev_feed, vd)
        )
        left_in.append(shifted(left, "space", 1))
        right_in.append(shifted(right, "space", -1))
        sent += [left, right]

    piece = orbitals // peers
    vd_share = lax.dynamic_slice_in_dim(vd_last, lax.axis_index("energy") * piece, piece, 0)
    vd_next = lax.all_gather(shifted(vd_share, "space", -1), "energy", axis=0, tiled=True)

    own_vd = product("rk,kj->rj", pick, vd).astype(BF)
    forward, inverse = transform_tables(energies, peers, share)
    real = (jnp.arange(batch, dtype=jnp.int32) < local).astype(F32)

    def padded(value):
        return jnp.pad(value, ((0, 0), (0, rows - value.shape[1]), (0, 0)))

    greens = [
        spread(by_peer(product("rk,bkj->brj", pick[c * rows : (c + 1) * rows], g).astype(BF)))
        for c in range(chunks)
    ]
    left_in[0], right_in[0], *sent = lax.optimization_barrier((left_in[0], right_in[0], *sent))
    sigmas, screens = [], []
    for c in range(chunks):
        part = slice(c * rows, (c + 1) * rows)
        same = product("rk,bkj->brj", own_vd[part], pd) + product(
            "rk,bjk->brj", own_vu[part], pu
        )
        one = product("rk,bkj->brj", own_vd[part], pu).astype(BF)
        total = product("brk,kj->brj", one, vd_next)
        total = total + real[:, None, None] * own_vu[part].astype(F32)
        total = total + padded(right_in[c]).astype(F32)
        total = total + product(
            "brk,kj->brj", (same + padded(left_in[c]).astype(F32)).astype(BF), vu
        )
        send_screen = by_peer(total.astype(BF))
        if c == 0:
            send_screen, *greens = lax.optimization_barrier((send_screen, *greens))
        shape = (peers * batch * share, orbitals)
        screen = spread(send_screen)
        if c + 1 < chunks:
            screen, left_in[c + 1], right_in[c + 1] = lax.optimization_barrier(
                (screen, left_in[c + 1], right_in[c + 1])
            )
        screens.append(screen)
        sigma = None
        if c + 1 < chunks:
            sigma = convolve(greens[c].reshape(shape), screen.reshape(shape), forward, inverse)
        sigmas.append(sigma)
    for c in range(chunks - 1):
        sigmas[c], screens[-1] = lax.optimization_barrier((sigmas[c], screens[-1]))
    sigmas[-1] = convolve(greens[-1].reshape(shape), screens[-1].reshape(shape), forward, inverse)
    backs = [spread(sigma.reshape(peers, batch, share, orbitals)) for sigma in sigmas]
    backs = [jnp.moveaxis(back, 0, 1).reshape(batch, rows, orbitals) for back in backs]
    out = None
    for c in range(chunks):
        term = product("rk,brj->bkj", pick[c * rows : (c + 1) * rows], backs[c])
        out = term if out is None else out + term
    return out.astype(BF).reshape(2, local, 1, orbitals, orbitals)


def solution(mesh):
    in_specs = (
        P(None, "energy", "space", None, None),
        P(None, "energy", "space", None, None),
        P(None, "energy", "space", None, None),
        P("space", None, None),
        P("space", None, None),
        P("space"),
        P("space", None),
    )
    out_specs = P(None, "energy", "space", None, None)
    return jax.shard_map(
        per_device, mesh=mesh, in_specs=in_specs, out_specs=out_specs, check_vma=False
    )
```

time: 172 us -> 187 us (1.087)
  waiting for transfers between devices: 60.3 us -> 34.2 us
  starting transfers between devices: 15.2 us -> 39.6 us
  Pallas kernels: 0 us -> 21.9 us
  matrix products: 44.8 us -> 57.6 us
  blocking collectives: 23.4 us -> 11 us
  local copies, waits for them, and re-layouts: 22.5 us -> 18.3 us
    ppermute x5 -> x7, waiting for transfers between devices: 46.9 us -> 17.4 us  [shifted(): return lax.ppermute(value, axis, pairs)]
    all_to_all x1 -> x0, blocking collectives: 23.4 us -> none  [spread(): lax.all_to_all(value, 'energy', split_axis=0, concat_axis=0, tiled=True)]
    pallas_call x0 -> x2, Pallas kernels: none -> 21.9 us  [convolve(): pl.pallas_call(convolve_kernel, out_shape=jax.ShapeDtypeStruct((count, co...]
    dot_general x10 -> x19, matrix products: 36.5 us -> 57.6 us  [product(): return jnp.einsum(form, left, right, preferred_element_type=F32)]
    all_to_all x2 -> x6, starting transfers between devices: 8.79 us -> 24.9 us  [spread(): lax.all_to_all(value, 'energy', split_axis=0, concat_axis=0, tiled=True)]
    all_gather x0 -> x1, blocking collectives: none -> 11 us  [per_device(): lax.all_gather(shifted(vd_share, 'space', -1), 'energy', axis=0, tiled=True)]
    ppermute x5 -> x7, starting transfers between devices: 6.36 us -> 14.7 us  [shifted(): return lax.ppermute(value, axis, pairs)]
    dot_general x3 -> x0, matrix products: 8.28 us -> none  [the longest x2 6.12 us: spectrum(): jnp.dot(forward, values.reshape(2 * energies, columns), preferred_element...]
  transfers between devices with their start and end apart: 7 -> 13, of which waited for: 4 -> 4; matrix products, arithmetic and copies ran while one was open for 28% -> 31% of each run, Pallas kernels for 0% -> 12%
where the time goes in v2:
time: 187 us; the launch traced here: 185 us
  matrix products  57.6 us (31%)
  starting transfers between devices  39.6 us (21%)
  waiting for transfers between devices  34.2 us (18%)
  Pallas kernels  21.9 us (12%)
  local copies, waits for them, and re-layouts  18.3 us (10%)
  blocking collectives  11 us (6%)
    dot_general x19, matrix products, product(): return jnp.einsum(form, left, right, preferred_element_type=F32)  57.6 us
    all_to_all x6, starting transfers between devices, spread(): lax.all_to_all(value, 'energy', split_axis=0, concat_axis=0, tiled=True)  24.9 us
    pallas_call x2, Pallas kernels, convolve(): pl.pallas_call(convolve_kernel, out_shape=jax.ShapeDtypeStruct((count, co...  21.9 us
    ppermute x7, waiting for transfers between devices, shifted(): return lax.ppermute(value, axis, pairs)  17.4 us
    all_to_all x6, waiting for transfers between devices, spread(): lax.all_to_all(value, 'energy', split_axis=0, concat_axis=0, tiled=True)  16.8 us
    ppermute x7, starting transfers between devices, shifted(): return lax.ppermute(value, axis, pairs)  14.7 us
    all_gather x1, blocking collectives, per_device(): lax.all_gather(shifted(vd_share, 'space', -1), 'energy', axis=0, tiled=True)  11 us
    reshape x4, local copies, waits for them, and re-layouts, by_peer(): return jnp.moveaxis(value.reshape(batch, peers, share, orbitals), 1, 0)  6.19 us
  transfers between devices with their start and end apart: 13, of which 4 were waited for; matrix products, arithmetic and copies ran while one was open for 31% of the time, Pallas kernels for 12%

profile of v2, /device:TPU:0, one launch (start us, length us, event | category | flops | bytes accessed | tf_op | source)
XLA Modules:
  0.0 185.3 jit_solution(4380264435986636781)
XLA Ops:
  0.0 5.0 %collective-permute-start = (s32[1,48]{1,0:T(1,128)}, s32[1,48]{1,0:T(1,128)S(1)}, u32[]{:S(2)}, u32[]{:S(2)}) collective-permute-start(s32[1,48]{1,0:T(1,128)} %param.15), channel_id=1, source_target_pairs={{0,3},{1,0},{2,1},{3,2},{4,7},{5,4},{6,5},{7,6},{8,11},{9,8},{10,9... | collective-permute-start | bytes 584 | tf_op jit(solution)/shard_map/ppermute | solution.py:21
  8.8 2.3 %convolution_convert_fusion.2 = bf16[128,8,384]{2,0,1:T(8,128)(2,1)S(1)} fusion(bf16[8,384,384]{2,1,0:T(8,128)(2,1)} %bitcast.187, pred[256,384]{1,0:T(32,128)(4,1)S(1)} %fusion.30), kind=kOutput, calls=%fused_computation.11 | convolution fusion | flops 302383104 | bytes 3194880 | tf_op jit(solution)/shard_map/rk,bkj->brj/dot_general | solution.py:25
  12.1 3.7 %all-to-all-start = ((bf16[8,8,16,384]{3,2,1,0:T(8,128)(2,1)}), bf16[8,8,16,384]{3,2,1,0:T(8,128)(2,1)S(1)}, u32[]{:S(2)}, u32[]{:S(2)}) async-start(bf16[8,8,16,384]{3,2,1,0:T(8,128)(2,1)} %bitcast.192), calls=%async_computation | async-start | bytes 1572864 | tf_op jit(solution)/shard_map/all_to_all | solution.py:105
  16.6 3.2 %convolution_convert_fusion.1 = bf16[128,8,384]{2,0,1:T(8,128)(2,1)} fusion(bf16[8,384,384]{2,1,0:T(8,128)(2,1)} %bitcast.188, pred[256,384]{1,0:T(32,128)(4,1)S(1)} %fusion.30), kind=kOutput, calls=%fused_computation.10 | convolution fusion | flops 302383104 | bytes 3194880 | tf_op jit(solution)/shard_map/rk,bkj->brj/dot_general | solution.py:25
  21.7 3.5 %fusion.64 = f32[128,8,384]{2,0,1:T(8,128)} fusion(bf16[8,384,384]{2,1,0:T(8,128)(2,1)} %bitcast.183, bf16[256,384]{1,0:T(8,128)(2,1)} %convolution_convert_fusion.11), kind=kOutput, calls=%fused_computation.85 | convolution fusion | flops 301989888 | bytes 4030464 | tf_op jit(solution)/shard_map/rk,bkj->brj/dot_general | solution.py:25
  28.0 4.0 %fusion.7 = f32[8,128,384]{2,1,0:T(8,128)} fusion(bf16[8,384,384]{2,1,0:T(8,128)(2,1)} %bitcast.184, bf16[1,384,384]{2,1,0:T(8,128)(2,1)} %param.12, bf16[240,384]{1,0:T(8,128)(2,1)} %collective-permute-done.1), kind=kOutput, calls=%fused_computation.24 | convolution fusion | flops 604372992 | bytes 4325376 | tf_op jit(solution)/shard_map/brk,kj->brj/dot_general | solution.py:25
  31.9 3.5 %add_convert_fusion.3 = bf16[8,128,384]{2,1,0:T(8,128)(2,1)} fusion(f32[8,128,384]{2,1,0:T(8,128)} %fusion.7, bf16[8,384,384]{2,1,0:T(8,128)(2,1)S(1)} %bitcast.175, bf16[1,384,384]{2,1,0:T(8,128)(2,1)S(1)} %copy-done.4, bf16[]{:T(256)} %bitcast.6, bf16[240,384]{1,0:T(8,128)(2,1)} %collective-permute-done.1), kind=kOutput, calls=%fused_computation.7 | convolution fusion | flops 605306880 | bytes 5112320 | tf_op jit(solution)/shard_map/brk,jk->brj/dot_general | solution.py:25
  35.6 3.6 %collective-permute-start.4 = (bf16[8,128,384]{2,1,0:T(8,128)(2,1)}, bf16[8,128,384]{2,1,0:T(8,128)(2,1)}, u32[]{:S(2)}, u32[]{:S(2)}) collective-permute-start(bf16[8,128,384]{2,1,0:T(8,128)(2,1)} %add_convert_fusion.3), channel_id=1, source_target_pairs={{0,3},{1,0},{2,1},{3,2},{4,7},{5,4},{6,5},{7,6},{8,11},{9,8},{10,9... | collective-permute-start | bytes 2359304 | tf_op jit(solution)/shard_map/ppermute | solution.py:21
  39.3 3.8 %fusion.13 = f32[8,112,384]{2,1,0:T(8,128)} fusion(bf16[8,384,384]{2,1,0:T(8,128)(2,1)} %bitcast.185, bf16[1,384,384]{2,1,0:T(8,128)(2,1)} %param.12, bf16[240,384]{1,0:T(8,128)(2,1)} %collective-permute-done.1), kind=kOutput, calls=%fused_computation.30 | convolution fusion | flops 528826368 | bytes 4116480 | tf_op jit(solution)/shard_map/brk,kj->brj/dot_general | solution.py:25
  43.1 3.3 %fusion.2 = bf16[8,112,384]{2,1,0:T(8,128)(2,1)} fusion(f32[8,112,384]{2,1,0:T(8,128)} %fusion.13, bf16[8,384,384]{2,1,0:T(8,128)(2,1)S(1)} %bitcast.177, bf16[1,384,384]{2,1,0:T(8,128)(2,1)S(1)} %copy-done.4, bf16[]{:T(256)} %bitcast.6, bf16[240,384]{1,0:T(8,128)(2,1)} %collective-permute-done.1), kind=kOutput, calls=%fused_computation.16 | convolution fusion | flops 529661952 | bytes 4805120 | tf_op jit(solution)/shard_map/brk,jk->brj/dot_general | solution.py:25
  46.4 2.5 %fusion.11 = bf16[8,112,384]{2,1,0:T(8,128)(2,1)} fusion(bf16[8,384,384]{2,1,0:T(8,128)(2,1)S(1)} %bitcast.176, bf16[240,384]{1,0:T(8,128)(2,1)} %copy-done.7), kind=kOutput, calls=%fused_computation.28 | convolution fusion | flops 264585216 | bytes 3133440 | tf_op jit(solution)/shard_map/rk,bkj->brj/dot_general | solution.py:25
  52.6 3.8 %collective-permute-start.6 = (bf16[8,112,384]{2,1,0:T(8,128)(2,1)}, bf16[8,112,384]{2,1,0:T(8,128)(2,1)}, u32[]{:S(2)}, u32[]{:S(2)}) collective-permute-start(bf16[8,112,384]{2,1,0:T(8,128)(2,1)} %fusion.2), channel_id=1, source_target_pairs={{0,3},{1,0},{2,1},{3,2},{4,7},{5,4},{6,5},{7,6},{8,11},{9,8},{10,9... | collective-permute-start | bytes 2064392 | tf_op jit(solution)/shard_map/ppermute | solution.py:21
  56.5 17.4 %collective-permute-done.2 = bf16[48,384]{1,0:T(8,128)(2,1)S(1)} collective-permute-done((bf16[48,384]{1,0:T(8,128)(2,1)S(1)}, bf16[48,384]{1,0:T(8,128)(2,1)S(1)}, u32[]{:S(2)}, u32[]{:S(2)}) %collective-permute-start.2) | collective-permute-done | bytes 36896 | tf_op jit(solution)/shard_map/ppermute | solution.py:21
  73.8 11.0 %all_gather.3 = bf16[384,384]{1,0:T(8,128)(2,1)} all-gather(bf16[48,384]{1,0:T(8,128)(2,1)S(1)} %collective-permute-done.2), channel_id=1, replica_groups=mesh['energy'=8,'space'=4] {'energy'}, dimensions={0}, use_global_device_ids=true | all-gather | bytes 331776 | tf_op jit(solution)/shard_map/all_gather | solution.py:138
  84.8 4.2 %all-to-all-start.1 = ((bf16[8,8,16,384]{3,2,1,0:T(8,128)(2,1)}), bf16[8,8,16,384]{3,2,1,0:T(8,128)(2,1)}, u32[]{:S(2)}, u32[]{:S(2)}) async-start(bf16[8,8,16,384]{3,2,1,0:T(8,128)(2,1)} %bitcast.193), calls=%async_computation.1 | async-start | bytes 1572864 | tf_op jit(solution)/shard_map/all_to_all | solution.py:105
  89.1 3.3 %fusion.4 = f32[8,128,384]{2,1,0:T(8,128)} fusion(bf16[8,384,384]{2,1,0:T(8,128)(2,1)S(1)} %bitcast.173, bf16[384,384]{1,0:T(8,128)(2,1)} %all_gather.3, bf16[256,384]{1,0:T(8,128)(2,1)} %convolution_convert_fusion.11), kind=kOutput, calls=%fused_computation.21 | convolution fusion | flops 604372992 | bytes 4325376 | tf_op jit(solution)/shard_map/brk,kj->brj/dot_general | solution.py:25
  92.3 4.6 %add_convert_fusion.2 = bf16[8,128,384]{2,1,0:T(8,128)(2,1)} fusion(bf16[8,128,384]{2,1,0:T(8,128)(2,1)} %collective-permute-done.4, f32[8,128,384]{2,1,0:T(8,128)} %fusion.4, bf16[8,128,384]{2,1,0:T(8,128)(2,1)} %collective-permute-done.3, f32[128,8,384]{2,0,1:T(8,128)} %fusion.64, bf16[8,384,384]{2,1,0:T(8,128)(2,1)S(1)} %bitcast.178, ...), kind=kOutput, calls=%fused_computation.6 | convolution fusion | flops 608059392 | bytes 8454688 | tf_op jit(solution)/shard_map/brk,kj->brj/dot_general | solution.py:25
  99.0 2.6 %all-to-all-done.1 = bf16[8,8,16,384]{3,2,1,0:T(8,128)(2,1)} async-done(((bf16[8,8,16,384]{3,2,1,0:T(8,128)(2,1)}), bf16[8,8,16,384]{3,2,1,0:T(8,128)(2,1)}, u32[]{:S(2)}, u32[]{:S(2)}) %all-to-all-start.1) | async-done | bytes 786464 | tf_op jit(solution)/shard_map/all_to_all | solution.py:105
  101.7 4.4 %all-to-all-start.2 = ((bf16[8,8,16,384]{3,2,1,0:T(8,128)(2,1)}), bf16[8,8,16,384]{3,2,1,0:T(8,128)(2,1)}, u32[]{:S(2)}, u32[]{:S(2)}) async-start(bf16[8,8,16,384]{3,2,1,0:T(8,128)(2,1)} %bitcast.194), calls=%async_computation.2 | async-start | bytes 1572864 | tf_op jit(solution)/shard_map/all_to_all | solution.py:105
  106.1 3.5 %fusion.65 = f32[128,8,384]{2,0,1:T(8,128)} fusion(bf16[8,384,384]{2,1,0:T(8,128)(2,1)} %bitcast.186, bf16[256,384]{1,0:T(8,128)(2,1)} %convolution_convert_fusion.11), kind=kOutput, calls=%fused_computation.86 | convolution fusion | flops 301989888 | bytes 4030464 | tf_op jit(solution)/shard_map/rk,bkj->brj/dot_general | solution.py:25
  109.6 3.3 %fusion.10 = f32[8,128,384]{2,1,0:T(8,128)} fusion(bf16[8,384,384]{2,1,0:T(8,128)(2,1)S(1)} %bitcast.179, bf16[384,384]{1,0:T(8,128)(2,1)} %all_gather.3, bf16[256,384]{1,0:T(8,128)(2,1)} %convolution_convert_fusion.11), kind=kOutput, calls=%fused_computation.27 | convolution fusion | flops 604372992 | bytes 4325376 | tf_op jit(solution)/shard_map/brk,kj->brj/dot_general | solution.py:25
  112.8 5.7 %all-to-all-done.2 = bf16[8,8,16,384]{3,2,1,0:T(8,128)(2,1)} async-done(((bf16[8,8,16,384]{3,2,1,0:T(8,128)(2,1)}), bf16[8,8,16,384]{3,2,1,0:T(8,128)(2,1)}, u32[]{:S(2)}, u32[]{:S(2)}) %all-to-all-start.2) | async-done | bytes 786464 | tf_op jit(solution)/shard_map/all_to_all | solution.py:105
  118.5 4.5 %add_convert_fusion.1 = bf16[8,128,384]{2,1,0:T(8,128)(2,1)} fusion(f32[8,128,384]{2,1,0:T(8,128)} %fusion.10, f32[128,8,384]{2,0,1:T(8,128)} %fusion.65, bf16[8,384,384]{2,1,0:T(8,128)(2,1)S(1)} %bitcast.180, bf16[8,112,384]{2,1,0:T(8,128)(2,1)} %collective-permute-done.5, bf16[8,112,384]{2,1,0:T(8,128)(2,1)} %collective-permute-done.6, ...), kind=kOutput, calls=%fused_computation.5 | convolution fusion | flops 608059392 | bytes 8258080 | tf_op jit(solution)/shard_map/brk,kj->brj/dot_general | solution.py:25
  125.2 4.2 %all-to-all-start.3 = ((bf16[8,8,16,384]{3,2,1,0:T(8,128)(2,1)}), bf16[8,8,16,384]{3,2,1,0:T(8,128)(2,1)}, u32[]{:S(2)}, u32[]{:S(2)}) async-start(bf16[8,8,16,384]{3,2,1,0:T(8,128)(2,1)} %bitcast.195), calls=%async_computation.3 | async-start | bytes 1572864 | tf_op jit(solution)/shard_map/all_to_all | solution.py:105
  131.0 10.6 %shard_map.91 = bf16[1024,384]{1,0:T(8,128)(2,1)S(1)} custom-call(bf16[1024,384]{1,0:T(8,128)(2,1)S(1)} %bitcast.181, bf16[1024,384]{1,0:T(8,128)(2,1)} %bitcast.36.screen_ref, bf16[1024,1024]{1,0:T(8,128)(2,1)S(1)} %copy-done.2, bf16[1024,1024]{1,0:T(8,128)(2,1)} %constant.22.clone.inverse_ref), custom_call_target="tpu_custom_call" | custom-call | flops 2415919104 | bytes 6553600 | tf_op jit(solution)/shard_map/pallas_call | solution.py:65
  142.5 4.2 %all-to-all-start.4 = ((bf16[8,8,16,384]{3,2,1,0:T(8,128)(2,1)}), bf16[8,8,16,384]{3,2,1,0:T(8,128)(2,1)}, u32[]{:S(2)}, u32[]{:S(2)}) async-start(bf16[8,8,16,384]{3,2,1,0:T(8,128)(2,1)} %bitcast.182), calls=%async_computation.4 | async-start | bytes 1572864 | tf_op jit(solution)/shard_map/all_to_all | solution.py:105
  148.3 11.3 %shard_map.92 = bf16[1024,384]{1,0:T(8,128)(2,1)} custom-call(bf16[1024,384]{1,0:T(8,128)(2,1)} %bitcast.46.green_ref, bf16[1024,384]{1,0:T(8,128)(2,1)} %bitcast.47.screen_ref, bf16[1024,1024]{1,0:T(8,128)(2,1)S(1)} %copy-done.3, bf16[1024,1024]{1,0:T(8,128)(2,1)} %constant.22.clone.inverse_ref), custom_call_target="tpu_custom_call" | custom-call | flops 2415919104 | bytes 6553600 | tf_op jit(solution)/shard_map/pallas_call | solution.py:65
  159.6 4.1 %all-to-all-start.5 = ((bf16[8,8,16,384]{3,2,1,0:T(8,128)(2,1)}), bf16[8,8,16,384]{3,2,1,0:T(8,128)(2,1)S(1)}, u32[]{:S(2)}, u32[]{:S(2)}) async-start(bf16[8,8,16,384]{3,2,1,0:T(8,128)(2,1)} %bitcast.48), calls=%async_computation.5 | async-start | bytes 1572864 | tf_op jit(solution)/shard_map/all_to_all | solution.py:105
  164.9 3.0 %fusion.45 = f32[8,384,384]{2,1,0:T(8,128)} fusion(bf16[8,128,384]{2,1,0:T(8,128)(2,1)S(1)} %bitcast.198, pred[256,384]{1,0:T(32,128)(4,1)S(1)} %fusion.30), kind=kOutput, calls=%fused_computation.68 | convolution fusion | flops 301989888 | bytes 5554176 | tf_op jit(solution)/shard_map/rk,brj->bkj/dot_general | solution.py:25
  167.9 8.4 %all-to-all-done.5 = bf16[8,8,16,384]{3,2,1,0:T(8,128)(2,1)S(1)} async-done(((bf16[8,8,16,384]{3,2,1,0:T(8,128)(2,1)}), bf16[8,8,16,384]{3,2,1,0:T(8,128)(2,1)S(1)}, u32[]{:S(2)}, u32[]{:S(2)}) %all-to-all-start.5) | async-done | bytes 786464 | tf_op jit(solution)/shard_map/all_to_all | solution.py:105
  176.4 4.6 %add_convert_fusion = bf16[8,384,384]{2,1,0:T(8,128)(2,1)} fusion(f32[8,384,384]{2,1,0:T(8,128)} %fusion.45, bf16[8,128,384]{2,1,0:T(8,128)(2,1)S(1)} %bitcast.199, pred[256,384]{1,0:T(32,128)(4,1)S(1)} %fusion.30), kind=kOutput, calls=%fused_computation | convolution fusion | flops 304349184 | bytes 7913472 | tf_op jit(solution)/shard_map/rk,brj->bkj/dot_general | solution.py:25
  181.0 4.3 %copy.43 = bf16[2,4,1,384,384]{4,3,2,1,0:T(8,128)(2,1)} copy(bf16[2,4,1,384,384]{3,4,1,0,2:T(8,128)(2,1)} %bitcast.189) | data formatting | bytes 4718592 | tf_op jit(solution)/shard_map/reshape | solution.py:188
  (52 shorter events, 23.2 us)
Async XLA Ops:
  0.0 25.8 %copy-start = (bf16[2,4,1,384,384]{4,3,2,1,0:T(8,128)(2,1)S(1)}, bf16[2,4,1,384,384]{4,3,2,1,0:T(8,128)(2,1)}, u32[]{:S(2)}) copy-start(bf16[2,4,1,384,384]{4,3,2,1,0:T(8,128)(2,1)} %param.11) | copy-start | bytes 7077892
  0.0 25.2 %collective-permute-start = (s32[1,48]{1,0:T(1,128)}, s32[1,48]{1,0:T(1,128)S(1)}, u32[]{:S(2)}, u32[]{:S(2)}) collective-permute-start(s32[1,48]{1,0:T(1,128)} %param.15), channel_id=1, source_target_pairs={{0,3},{1,0},{2,1},{3,2},{4,7},{5,4},{6,5},{7,6},{8,11},{9,8},{10,9... | collective-permute-start | bytes 584 | tf_op jit(solution)/shard_map/ppermute | solution.py:21
  8.0 7.8 %copy-start.6 = (bf16[256,384]{1,0:T(8,128)(2,1)}, bf16[256,384]{1,0:T(8,128)(2,1)S(1)}, u32[]{:S(2)}) copy-start(bf16[256,384]{1,0:T(8,128)(2,1)S(1)} %convolution_convert_fusion.10) | copy-start | bytes 589828
  8.7 19.2 %collective-permute-start.1 = (bf16[240,384]{1,0:T(8,128)(2,1)}, bf16[240,384]{1,0:T(8,128)(2,1)}, u32[]{:S(2)}, u32[]{:S(2)}) collective-permute-start(bf16[240,384]{1,0:T(8,128)(2,1)} %slice.54), channel_id=1, source_target_pairs={{0,1},{1,2},{2,3},{3,0},{4,5},{5,6},{6,7},{7,4},{8,9},{9,10},{10,1... | collective-permute-start | bytes 552968 | tf_op jit(solution)/shard_map/ppermute | solution.py:21
  12.1 72.8 %all-to-all-start = ((bf16[8,8,16,384]{3,2,1,0:T(8,128)(2,1)}), bf16[8,8,16,384]{3,2,1,0:T(8,128)(2,1)S(1)}, u32[]{:S(2)}, u32[]{:S(2)}) async-start(bf16[8,8,16,384]{3,2,1,0:T(8,128)(2,1)} %bitcast.192), calls=%async_computation | async-start | bytes 1572864 | tf_op jit(solution)/shard_map/all_to_all | solution.py:105
  19.7 5.8 %copy-start.4 = (bf16[1,384,384]{2,1,0:T(8,128)(2,1)S(1)}, bf16[1,384,384]{2,1,0:T(8,128)(2,1)}, u32[]{:S(2)}) copy-start(bf16[1,384,384]{2,1,0:T(8,128)(2,1)} %param.13) | copy-start | bytes 884740
  25.8 0.7 copy-start.7
  35.4 56.9 %collective-permute-start.3 = (bf16[8,128,384]{2,1,0:T(8,128)(2,1)}, bf16[8,128,384]{2,1,0:T(8,128)(2,1)}, u32[]{:S(2)}, u32[]{:S(2)}) collective-permute-start(bf16[8,128,384]{2,1,0:T(8,128)(2,1)} %fusion.5), channel_id=1, source_target_pairs={{0,1},{1,2},{2,3},{3,0},{4,5},{5,6},{6,7},{7,4},{8,9},{9,10},{10,1... | collective-permute-start | bytes 2359304 | tf_op jit(solution)/shard_map/ppermute | solution.py:21
  35.6 56.7 %collective-permute-start.4 = (bf16[8,128,384]{2,1,0:T(8,128)(2,1)}, bf16[8,128,384]{2,1,0:T(8,128)(2,1)}, u32[]{:S(2)}, u32[]{:S(2)}) collective-permute-start(bf16[8,128,384]{2,1,0:T(8,128)(2,1)} %add_convert_fusion.3), channel_id=1, source_target_pairs={{0,3},{1,0},{2,1},{3,2},{4,7},{5,4},{6,5},{7,6},{8,11},{9,8},{10,9... | collective-permute-start | bytes 2359304 | tf_op jit(solution)/shard_map/ppermute | solution.py:21
  46.4 5.3 %copy-start.5 = (bf16[128,8,384]{2,0,1:T(8,128)(2,1)S(1)}, bf16[128,8,384]{2,0,1:T(8,128)(2,1)}, u32[]{:S(2)}) copy-start(bf16[128,8,384]{2,0,1:T(8,128)(2,1)} %convolution_convert_fusion.1) | copy-start | bytes 2359300
  49.6 24.2 %collective-permute-start.2 = (bf16[48,384]{1,0:T(8,128)(2,1)S(1)}, bf16[48,384]{1,0:T(8,128)(2,1)S(1)}, u32[]{:S(2)}, u32[]{:S(2)}) collective-permute-start(bf16[48,384]{1,0:T(8,128)(2,1)S(1)} %constant_dynamic-slice_fusion), channel_id=1, source_target_pairs={{0,3},{1,0},{2,1},{3,2},{4,7},{5,4},{6,5},{7,6},{8,11},{9,8},{10,9... | collective-permute-start | bytes 110600 | tf_op jit(solution)/shard_map/ppermute | solution.py:21
  52.6 60.2 %collective-permute-start.5 = (bf16[8,112,384]{2,1,0:T(8,128)(2,1)}, bf16[8,112,384]{2,1,0:T(8,128)(2,1)}, u32[]{:S(2)}, u32[]{:S(2)}) collective-permute-start(bf16[8,112,384]{2,1,0:T(8,128)(2,1)} %fusion.11), channel_id=1, source_target_pairs={{0,1},{1,2},{2,3},{3,0},{4,5},{5,6},{6,7},{7,4},{8,9},{9,10},{10,1... | collective-permute-start | bytes 2064392 | tf_op jit(solution)/shard_map/ppermute | solution.py:21
  52.6 60.2 %collective-permute-start.6 = (bf16[8,112,384]{2,1,0:T(8,128)(2,1)}, bf16[8,112,384]{2,1,0:T(8,128)(2,1)}, u32[]{:S(2)}, u32[]{:S(2)}) collective-permute-start(bf16[8,112,384]{2,1,0:T(8,128)(2,1)} %fusion.2), channel_id=1, source_target_pairs={{0,3},{1,0},{2,1},{3,2},{4,7},{5,4},{6,5},{7,6},{8,11},{9,8},{10,9... | collective-permute-start | bytes 2064392 | tf_op jit(solution)/shard_map/ppermute | solution.py:21
  84.8 16.8 %all-to-all-start.1 = ((bf16[8,8,16,384]{3,2,1,0:T(8,128)(2,1)}), bf16[8,8,16,384]{3,2,1,0:T(8,128)(2,1)}, u32[]{:S(2)}, u32[]{:S(2)}) async-start(bf16[8,8,16,384]{3,2,1,0:T(8,128)(2,1)} %bitcast.193), calls=%async_computation.1 | async-start | bytes 1572864 | tf_op jit(solution)/shard_map/all_to_all | solution.py:105
  101.7 16.8 %all-to-all-start.2 = ((bf16[8,8,16,384]{3,2,1,0:T(8,128)(2,1)}), bf16[8,8,16,384]{3,2,1,0:T(8,128)(2,1)}, u32[]{:S(2)}, u32[]{:S(2)}) async-start(bf16[8,8,16,384]{3,2,1,0:T(8,128)(2,1)} %bitcast.194), calls=%async_computation.2 | async-start | bytes 1572864 | tf_op jit(solution)/shard_map/all_to_all | solution.py:105
  125.2 17.3 %all-to-all-start.3 = ((bf16[8,8,16,384]{3,2,1,0:T(8,128)(2,1)}), bf16[8,8,16,384]{3,2,1,0:T(8,128)(2,1)}, u32[]{:S(2)}, u32[]{:S(2)}) async-start(bf16[8,8,16,384]{3,2,1,0:T(8,128)(2,1)} %bitcast.195), calls=%async_computation.3 | async-start | bytes 1572864 | tf_op jit(solution)/shard_map/all_to_all | solution.py:105
  129.4 1.6 copy-start.2
  141.6 0.9 copy-start.1
  142.5 17.1 %all-to-all-start.4 = ((bf16[8,8,16,384]{3,2,1,0:T(8,128)(2,1)}), bf16[8,8,16,384]{3,2,1,0:T(8,128)(2,1)}, u32[]{:S(2)}, u32[]{:S(2)}) async-start(bf16[8,8,16,384]{3,2,1,0:T(8,128)(2,1)} %bitcast.182), calls=%async_computation.4 | async-start | bytes 1572864 | tf_op jit(solution)/shard_map/all_to_all | solution.py:105
  146.7 1.6 copy-start.3
  159.6 16.7 %all-to-all-start.5 = ((bf16[8,8,16,384]{3,2,1,0:T(8,128)(2,1)}), bf16[8,8,16,384]{3,2,1,0:T(8,128)(2,1)S(1)}, u32[]{:S(2)}, u32[]{:S(2)}) async-start(bf16[8,8,16,384]{3,2,1,0:T(8,128)(2,1)} %bitcast.48), calls=%async_computation.5 | async-start | bytes 1572864 | tf_op jit(solution)/shard_map/all_to_all | solution.py:105

commit v3 on v2

--- a/solution.py
+++ b/solution.py
@@ -59,7 +59,7 @@
 
 def convolve(green, screen, forward, inverse):
     count, columns = green.shape
-    tile = 128 if columns % 128 == 0 else columns
+    tile = columns
     block = pl.BlockSpec((count, tile), lambda j: (0, j))
     table = pl.BlockSpec((count, count), lambda j: (0, 0))
     return pl.pallas_call(
@@ -114,6 +114,7 @@
     own_vu = product("rk,kj->rj", pick, vu).astype(BF)
     prev_vu = shifted(own_vu[: LIVE * width], "space", 1)
     present_next = shifted(element_present, "space", -1)
+    vd_next, present_next = lax.optimization_barrier((shifted(vd, "space", -1), present_next))
     pick_next = selection(present_next[0], orbitals, LIVE * width)
     next_vu = product("rk,jk->rj", pick_next, vu).astype(BF)
 
@@ -126,18 +127,14 @@
             "brk,kj->brj", product("rk,bkj->brj", prev_feed[part], pd).astype(BF), vd
         ) + product("brk,jk->brj", product("rk,bkj->brj", prev_feed[part], pu).astype(BF), vu)
         right = right.astype(BF)
-        left, right, feed, prev_feed, vd_last = lax.optimization_barrier(
-            (left, right, feed, prev_feed, vd)
+        left, right, feed, prev_feed, pick, vd_late = lax.optimization_barrier(
+            (left, right, feed, prev_feed, pick, vd)
         )
         left_in.append(shifted(left, "space", 1))
         right_in.append(shifted(right, "space", -1))
         sent += [left, right]
 
-    piece = orbitals // peers
-    vd_share = lax.dynamic_slice_in_dim(vd_last, lax.axis_index("energy") * piece, piece, 0)
-    vd_next = lax.all_gather(shifted(vd_share, "space", -1), "energy", axis=0, tiled=True)
-
-    own_vd = product("rk,kj->rj", pick, vd).astype(BF)
+    own_vd = product("rk,kj->rj", pick, vd_late).astype(BF)
     forward, inverse = transform_tables(energies, peers, share)
     real = (jnp.arange(batch, dtype=jnp.int32) < local).astype(F32)
 

time: 187 us -> 180 us (0.963)
  waiting for transfers between devices: 34.2 us -> 53.8 us
  blocking collectives: 11 us -> 0 us
  Pallas kernels: 21.9 us -> 11.8 us
  matrix products: 57.6 us -> 54.7 us
  local copies, waits for them, and re-layouts: 18.3 us -> 16.3 us
    ppermute x7, waiting for transfers between devices: 17.4 us -> 35 us  [shifted(): return lax.ppermute(value, axis, pairs)]
    all_gather x1 -> x0, blocking collectives: 11 us -> none  [per_device(): lax.all_gather(shifted(vd_share, 'space', -1), 'energy', axis=0, tiled=True)]
    pallas_call x2, Pallas kernels: 21.9 us -> 11.8 us  [convolve(): pl.pallas_call(convolve_kernel, out_shape=jax.ShapeDtypeStruct((count, co...]
    dot_general x19, matrix products: 57.6 us -> 54.7 us  [product(): return jnp.einsum(form, left, right, preferred_element_type=F32)]
    all_to_all x6, waiting for transfers between devices: 16.8 us -> 18.8 us  [spread(): lax.all_to_all(value, 'energy', split_axis=0, concat_axis=0, tiled=True)]
    unnamed x16 -> x24, local copies, waits for them, and re-layouts: 4.74 us -> 4.17 us
  transfers between devices with their start and end apart: 13 -> 13, of which waited for: 4 -> 7; matrix products, arithmetic and copies ran while one was open for 31% -> 21% of each run, Pallas kernels for 12% -> 7%
where the time goes in v3:
time: 180 us; the launch traced here: 178 us
  matrix products  54.7 us (30%)
  waiting for transfers between devices  53.8 us (30%)
  starting transfers between devices  39.1 us (22%)
  local copies, waits for them, and re-layouts  16.3 us (9%)
  Pallas kernels  11.8 us (7%)
  other arithmetic  1.82 us (1%)
    dot_general x19, matrix products, product(): return jnp.einsum(form, left, right, preferred_element_type=F32)  54.7 us
    ppermute x7, waiting for transfers between devices, shifted(): return lax.ppermute(value, axis, pairs)  35 us
    all_to_all x6, starting transfers between devices, spread(): lax.all_to_all(value, 'energy', split_axis=0, concat_axis=0, tiled=True)  24.3 us
    all_to_all x6, waiting for transfers between devices, spread(): lax.all_to_all(value, 'energy', split_axis=0, concat_axis=0, tiled=True)  18.8 us
    ppermute x7, starting transfers between devices, shifted(): return lax.ppermute(value, axis, pairs)  14.8 us
    pallas_call x2, Pallas kernels, convolve(): pl.pallas_call(convolve_kernel, out_shape=jax.ShapeDtypeStruct((count, co...  11.8 us
    reshape x4, local copies, waits for them, and re-layouts, by_peer(): return jnp.moveaxis(value.reshape(batch, peers, share, orbitals), 1, 0)  6.21 us
    reshape x1, local copies, waits for them, and re-layouts, per_device(): return out.astype(BF).reshape(2, local, 1, orbitals, orbitals)  4.27 us
  transfers between devices with their start and end apart: 13, of which 7 were waited for; matrix products, arithmetic and copies ran while one was open for 21% of the time, Pallas kernels for 7%

profile of v3, /device:TPU:0, one launch (start us, length us, event | category | flops | bytes accessed | tf_op | source)
XLA Modules:
  0.0 178.4 jit_solution(17905071550012222791)
XLA Ops:
  0.0 5.0 %collective-permute-start = (bf16[384,384]{1,0:T(8,128)(2,1)}, bf16[384,384]{1,0:T(8,128)(2,1)S(1)}, u32[]{:S(2)}, u32[]{:S(2)}) collective-permute-start(bf16[384,384]{1,0:T(8,128)(2,1)} %bitcast.202), channel_id=1, source_target_pairs={{0,3},{1,0},{2,1},{3,2},{4,7},{5,4},{6,5},{7,6},{8,11},{9,8},{10,9... | collective-permute-start | bytes 884744 | tf_op jit(solution)/shard_map/ppermute | solution.py:21
  11.0 5.4 %collective-permute-done.2 = bf16[240,384]{1,0:T(8,128)(2,1)S(1)} collective-permute-done((bf16[240,384]{1,0:T(8,128)(2,1)S(1)}, bf16[240,384]{1,0:T(8,128)(2,1)S(1)}, u32[]{:S(2)}, u32[]{:S(2)}) %collective-permute-start.2) | collective-permute-done | bytes 184352 | tf_op jit(solution)/shard_map/ppermute | solution.py:21
  16.4 3.9 %fusion.5 = f32[8,128,384]{2,1,0:T(8,128)} fusion(bf16[8,384,384]{2,1,0:T(8,128)(2,1)} %bitcast.185, bf16[1,384,384]{2,1,0:T(8,128)(2,1)} %param.12, bf16[240,384]{1,0:T(8,128)(2,1)S(1)} %collective-permute-done.2), kind=kOutput, calls=%fused_computation.22 | convolution fusion | flops 604372992 | bytes 4325376 | tf_op jit(solution)/shard_map/brk,kj->brj/dot_general | solution.py:25
  20.3 3.5 %add_convert_fusion.3 = bf16[8,128,384]{2,1,0:T(8,128)(2,1)} fusion(f32[8,128,384]{2,1,0:T(8,128)} %fusion.5, bf16[8,384,384]{2,1,0:T(8,128)(2,1)S(1)} %bitcast.176, bf16[1,384,384]{2,1,0:T(8,128)(2,1)S(1)} %copy-done.4, bf16[]{:T(256)} %bitcast.2, bf16[240,384]{1,0:T(8,128)(2,1)S(1)} %collective-permute-done.2), kind=kOutput, calls=%fused_computation.7 | convolution fusion | flops 605306880 | bytes 5111810 | tf_op jit(solution)/shard_map/brk,jk->brj/dot_general | solution.py:25
  27.5 3.8 %fusion.13 = f32[8,112,384]{2,1,0:T(8,128)} fusion(bf16[8,384,384]{2,1,0:T(8,128)(2,1)} %bitcast.186, bf16[1,384,384]{2,1,0:T(8,128)(2,1)S(1)} %copy-done.8, bf16[240,384]{1,0:T(8,128)(2,1)S(1)} %collective-permute-done.2), kind=kOutput, calls=%fused_computation.30 | convolution fusion | flops 528826368 | bytes 4116480 | tf_op jit(solution)/shard_map/brk,kj->brj/dot_general | solution.py:25
  31.2 3.3 %fusion.2 = bf16[8,112,384]{2,1,0:T(8,128)(2,1)} fusion(f32[8,112,384]{2,1,0:T(8,128)} %fusion.13, bf16[8,384,384]{2,1,0:T(8,128)(2,1)S(1)} %bitcast.178, bf16[1,384,384]{2,1,0:T(8,128)(2,1)S(1)} %copy-done.4, bf16[]{:T(256)} %bitcast.2, bf16[240,384]{1,0:T(8,128)(2,1)S(1)} %collective-permute-done.2), kind=kOutput, calls=%fused_computation.16 | convolution fusion | flops 529661952 | bytes 4804610 | tf_op jit(solution)/shard_map/brk,jk->brj/dot_general | solution.py:25
  34.6 2.2 %convolution_convert_fusion.2 = bf16[128,8,384]{2,0,1:T(8,128)(2,1)S(1)} fusion(bf16[8,384,384]{2,1,0:T(8,128)(2,1)} %bitcast.189, bf16[256,384]{1,0:T(8,128)(2,1)S(1)} %fusion.31), kind=kOutput, calls=%fused_computation.11 | convolution fusion | flops 302383104 | bytes 3244032 | tf_op jit(solution)/shard_map/rk,bkj->brj/dot_general | solution.py:25
  37.8 3.7 %all-to-all-start = ((bf16[8,8,16,384]{3,2,1,0:T(8,128)(2,1)}), bf16[8,8,16,384]{3,2,1,0:T(8,128)(2,1)S(1)}, u32[]{:S(2)}, u32[]{:S(2)}) async-start(bf16[8,8,16,384]{3,2,1,0:T(8,128)(2,1)} %bitcast.195), calls=%async_computation | async-start | bytes 1572864 | tf_op jit(solution)/shard_map/all_to_all | solution.py:105
  41.5 2.4 %convolution_convert_fusion.1 = bf16[128,8,384]{2,0,1:T(8,128)(2,1)S(1)} fusion(bf16[8,384,384]{2,1,0:T(8,128)(2,1)} %bitcast.190, bf16[256,384]{1,0:T(8,128)(2,1)} %copy-done.5), kind=kOutput, calls=%fused_computation.10 | convolution fusion | flops 302383104 | bytes 3244032 | tf_op jit(solution)/shard_map/rk,bkj->brj/dot_general | solution.py:25
  45.6 2.2 %collective-permute-start.4 = (bf16[8,128,384]{2,1,0:T(8,128)(2,1)}, bf16[8,128,384]{2,1,0:T(8,128)(2,1)}, u32[]{:S(2)}, u32[]{:S(2)}) collective-permute-start(bf16[8,128,384]{2,1,0:T(8,128)(2,1)} %add_convert_fusion.3), channel_id=1, source_target_pairs={{0,3},{1,0},{2,1},{3,2},{4,7},{5,4},{6,5},{7,6},{8,11},{9,8},{10,9... | collective-permute-start | bytes 2359304 | tf_op jit(solution)/shard_map/ppermute | solution.py:21
  48.8 3.8 %collective-permute-start.6 = (bf16[8,112,384]{2,1,0:T(8,128)(2,1)}, bf16[8,112,384]{2,1,0:T(8,128)(2,1)}, u32[]{:S(2)}, u32[]{:S(2)}) collective-permute-start(bf16[8,112,384]{2,1,0:T(8,128)(2,1)} %fusion.2), channel_id=1, source_target_pairs={{0,3},{1,0},{2,1},{3,2},{4,7},{5,4},{6,5},{7,6},{8,11},{9,8},{10,9... | collective-permute-start | bytes 2064392 | tf_op jit(solution)/shard_map/ppermute | solution.py:21
  53.5 3.3 %fusion.8 = f32[8,128,384]{2,1,0:T(8,128)} fusion(bf16[8,384,384]{2,1,0:T(8,128)(2,1)S(1)} %bitcast.179, bf16[384,384]{1,0:T(8,128)(2,1)} %copy-done.11, bf16[256,384]{1,0:T(8,128)(2,1)} %convolution_convert_fusion.10), kind=kOutput, calls=%fused_computation.25 | convolution fusion | flops 604372992 | bytes 4325376 | tf_op jit(solution)/shard_map/brk,kj->brj/dot_general | solution.py:25
  56.8 4.2 %all-to-all-start.1 = ((bf16[8,8,16,384]{3,2,1,0:T(8,128)(2,1)}), bf16[8,8,16,384]{3,2,1,0:T(8,128)(2,1)}, u32[]{:S(2)}, u32[]{:S(2)}) async-start(bf16[8,8,16,384]{3,2,1,0:T(8,128)(2,1)} %bitcast.194), calls=%async_computation.1 | async-start | bytes 1572864 | tf_op jit(solution)/shard_map/all_to_all | solution.py:105
  61.0 3.5 %fusion.76 = f32[128,8,384]{2,0,1:T(8,128)} fusion(bf16[8,384,384]{2,1,0:T(8,128)(2,1)} %bitcast.187, bf16[256,384]{1,0:T(8,128)(2,1)} %convolution_convert_fusion.10), kind=kOutput, calls=%fused_computation.94 | convolution fusion | flops 301989888 | bytes 4030464 | tf_op jit(solution)/shard_map/rk,bkj->brj/dot_general | solution.py:25
  66.5 16.9 %collective-permute-done.4 = bf16[8,128,384]{2,1,0:T(8,128)(2,1)} collective-permute-done((bf16[8,128,384]{2,1,0:T(8,128)(2,1)}, bf16[8,128,384]{2,1,0:T(8,128)(2,1)}, u32[]{:S(2)}, u32[]{:S(2)}) %collective-permute-start.4) | collective-permute-done | bytes 786464 | tf_op jit(solution)/shard_map/ppermute | solution.py:21
  83.3 4.6 %add_convert_fusion.2 = bf16[8,128,384]{2,1,0:T(8,128)(2,1)} fusion(bf16[8,128,384]{2,1,0:T(8,128)(2,1)} %collective-permute-done.4, f32[8,128,384]{2,1,0:T(8,128)} %fusion.8, bf16[8,128,384]{2,1,0:T(8,128)(2,1)} %collective-permute-done.3, f32[128,8,384]{2,0,1:T(8,128)} %fusion.76, bf16[8,384,384]{2,1,0:T(8,128)(2,1)S(1)} %bitcast.180, ...), kind=kOutput, calls=%fused_computation.6 | convolution fusion | flops 608059392 | bytes 8454688 | tf_op jit(solution)/shard_map/brk,kj->brj/dot_general | solution.py:25
  90.0 4.4 %all-to-all-start.2 = ((bf16[8,8,16,384]{3,2,1,0:T(8,128)(2,1)}), bf16[8,8,16,384]{3,2,1,0:T(8,128)(2,1)}, u32[]{:S(2)}, u32[]{:S(2)}) async-start(bf16[8,8,16,384]{3,2,1,0:T(8,128)(2,1)} %bitcast.196), calls=%async_computation.2 | async-start | bytes 1572864 | tf_op jit(solution)/shard_map/all_to_all | solution.py:105
  94.4 3.5 %fusion.77 = f32[128,8,384]{2,0,1:T(8,128)} fusion(bf16[8,384,384]{2,1,0:T(8,128)(2,1)} %bitcast.188, bf16[256,384]{1,0:T(8,128)(2,1)} %convolution_convert_fusion.10), kind=kOutput, calls=%fused_computation.95 | convolution fusion | flops 301989888 | bytes 4030464 | tf_op jit(solution)/shard_map/rk,bkj->brj/dot_general | solution.py:25
  97.9 3.3 %fusion.10 = f32[8,128,384]{2,1,0:T(8,128)} fusion(bf16[8,384,384]{2,1,0:T(8,128)(2,1)S(1)} %bitcast.181, bf16[384,384]{1,0:T(8,128)(2,1)} %copy-done.11, bf16[256,384]{1,0:T(8,128)(2,1)} %convolution_convert_fusion.10), kind=kOutput, calls=%fused_computation.27 | convolution fusion | flops 604372992 | bytes 4325376 | tf_op jit(solution)/shard_map/brk,kj->brj/dot_general | solution.py:25
  101.2 10.7 %collective-permute-done.6 = bf16[8,112,384]{2,1,0:T(8,128)(2,1)} collective-permute-done((bf16[8,112,384]{2,1,0:T(8,128)(2,1)}, bf16[8,112,384]{2,1,0:T(8,128)(2,1)}, u32[]{:S(2)}, u32[]{:S(2)}) %collective-permute-start.6) | collective-permute-done | bytes 688160 | tf_op jit(solution)/shard_map/ppermute | solution.py:21
  111.9 4.5 %add_convert_fusion.1 = bf16[8,128,384]{2,1,0:T(8,128)(2,1)} fusion(f32[8,128,384]{2,1,0:T(8,128)} %fusion.10, f32[128,8,384]{2,0,1:T(8,128)} %fusion.77, bf16[8,384,384]{2,1,0:T(8,128)(2,1)S(1)} %bitcast.182, bf16[8,112,384]{2,1,0:T(8,128)(2,1)} %collective-permute-done.5, bf16[8,112,384]{2,1,0:T(8,128)(2,1)} %collective-permute-done.6, ...), kind=kOutput, calls=%fused_computation.5 | convolution fusion | flops 608059392 | bytes 8258080 | tf_op jit(solution)/shard_map/brk,kj->brj/dot_general | solution.py:25
  118.6 4.2 %all-to-all-start.3 = ((bf16[8,8,16,384]{3,2,1,0:T(8,128)(2,1)}), bf16[8,8,16,384]{3,2,1,0:T(8,128)(2,1)}, u32[]{:S(2)}, u32[]{:S(2)}) async-start(bf16[8,8,16,384]{3,2,1,0:T(8,128)(2,1)} %bitcast.197), calls=%async_computation.3 | async-start | bytes 1572864 | tf_op jit(solution)/shard_map/all_to_all | solution.py:105
  124.4 5.3 %shard_map.91 = bf16[1024,384]{1,0:T(8,128)(2,1)S(1)} custom-call(bf16[1024,384]{1,0:T(8,128)(2,1)S(1)} %bitcast.183, bf16[1024,384]{1,0:T(8,128)(2,1)} %bitcast.36.screen_ref, bf16[1024,1024]{1,0:T(8,128)(2,1)S(1)} %copy-done.2, bf16[1024,1024]{1,0:T(8,128)(2,1)} %constant.12.clone.inverse_ref), custom_call_target="tpu_custom_call" | custom-call | flops 2415919104 | bytes 6553600 | tf_op jit(solution)/shard_map/pallas_call | solution.py:65
  130.6 4.8 %all-to-all-done.3 = bf16[8,8,16,384]{3,2,1,0:T(8,128)(2,1)} async-done(((bf16[8,8,16,384]{3,2,1,0:T(8,128)(2,1)}), bf16[8,8,16,384]{3,2,1,0:T(8,128)(2,1)}, u32[]{:S(2)}, u32[]{:S(2)}) %all-to-all-start.3) | async-done | bytes 786464 | tf_op jit(solution)/shard_map/all_to_all | solution.py:105
  135.4 3.5 %all-to-all-start.4 = ((bf16[8,8,16,384]{3,2,1,0:T(8,128)(2,1)}), bf16[8,8,16,384]{3,2,1,0:T(8,128)(2,1)S(1)}, u32[]{:S(2)}, u32[]{:S(2)}) async-start(bf16[8,8,16,384]{3,2,1,0:T(8,128)(2,1)} %bitcast.184), calls=%async_computation.4 | async-start | bytes 1572864 | tf_op jit(solution)/shard_map/all_to_all | solution.py:105
  140.6 6.5 %shard_map.92 = bf16[1024,384]{1,0:T(8,128)(2,1)} custom-call(bf16[1024,384]{1,0:T(8,128)(2,1)} %bitcast.46.green_ref, bf16[1024,384]{1,0:T(8,128)(2,1)} %bitcast.47.screen_ref, bf16[1024,1024]{1,0:T(8,128)(2,1)S(1)} %copy-done.3, bf16[1024,1024]{1,0:T(8,128)(2,1)} %constant.12.clone.inverse_ref), custom_call_target="tpu_custom_call" | custom-call | flops 2415919104 | bytes 6553600 | tf_op jit(solution)/shard_map/pallas_call | solution.py:65
  147.1 4.5 %all-to-all-done.4 = bf16[8,8,16,384]{3,2,1,0:T(8,128)(2,1)S(1)} async-done(((bf16[8,8,16,384]{3,2,1,0:T(8,128)(2,1)}), bf16[8,8,16,384]{3,2,1,0:T(8,128)(2,1)S(1)}, u32[]{:S(2)}, u32[]{:S(2)}) %all-to-all-start.4) | async-done | bytes 786464 | tf_op jit(solution)/shard_map/all_to_all | solution.py:105
  151.5 4.2 %all-to-all-start.5 = ((bf16[8,8,16,384]{3,2,1,0:T(8,128)(2,1)}), bf16[8,8,16,384]{3,2,1,0:T(8,128)(2,1)}, u32[]{:S(2)}, u32[]{:S(2)}) async-start(bf16[8,8,16,384]{3,2,1,0:T(8,128)(2,1)} %bitcast.48), calls=%async_computation.5 | async-start | bytes 1572864 | tf_op jit(solution)/shard_map/all_to_all | solution.py:105
  155.8 2.9 %fusion.53 = f32[8,384,384]{2,1,0:T(8,128)} fusion(bf16[8,128,384]{2,1,0:T(8,128)(2,1)S(1)} %bitcast.200, bf16[256,384]{1,0:T(8,128)(2,1)S(1)} %copy-done.7), kind=kOutput, calls=%fused_computation.76 | convolution fusion | flops 301989888 | bytes 5603328 | tf_op jit(solution)/shard_map/rk,brj->bkj/dot_general | solution.py:25
  158.8 9.6 %all-to-all-done.5 = bf16[8,8,16,384]{3,2,1,0:T(8,128)(2,1)} async-done(((bf16[8,8,16,384]{3,2,1,0:T(8,128)(2,1)}), bf16[8,8,16,384]{3,2,1,0:T(8,128)(2,1)}, u32[]{:S(2)}, u32[]{:S(2)}) %all-to-all-start.5) | async-done | bytes 786464 | tf_op jit(solution)/shard_map/all_to_all | solution.py:105
  169.6 4.6 %add_convert_fusion = bf16[8,384,384]{2,1,0:T(8,128)(2,1)} fusion(f32[8,384,384]{2,1,0:T(8,128)} %fusion.53, bf16[8,128,384]{2,1,0:T(8,128)(2,1)S(1)} %bitcast.201, bf16[256,384]{1,0:T(8,128)(2,1)S(1)} %copy-done.7), kind=kOutput, calls=%fused_computation | convolution fusion | flops 304349184 | bytes 7962624 | tf_op jit(solution)/shard_map/rk,brj->bkj/dot_general | solution.py:25
  174.2 4.3 %copy.43 = bf16[2,4,1,384,384]{4,3,2,1,0:T(8,128)(2,1)} copy(bf16[2,4,1,384,384]{3,4,1,0,2:T(8,128)(2,1)} %bitcast.191) | data formatting | bytes 4718592 | tf_op jit(solution)/shard_map/reshape | solution.py:185
  (58 shorter events, 25.1 us)
Async XLA Ops:
  0.0 20.3 %copy-start = (bf16[2,4,1,384,384]{4,3,2,1,0:T(8,128)(2,1)S(1)}, bf16[2,4,1,384,384]{4,3,2,1,0:T(8,128)(2,1)}, u32[]{:S(2)}) copy-start(bf16[2,4,1,384,384]{4,3,2,1,0:T(8,128)(2,1)} %param.11) | copy-start | bytes 7077892
  0.0 23.8 %collective-permute-start = (bf16[384,384]{1,0:T(8,128)(2,1)}, bf16[384,384]{1,0:T(8,128)(2,1)S(1)}, u32[]{:S(2)}, u32[]{:S(2)}) collective-permute-start(bf16[384,384]{1,0:T(8,128)(2,1)} %bitcast.202), channel_id=1, source_target_pairs={{0,3},{1,0},{2,1},{3,2},{4,7},{5,4},{6,5},{7,6},{8,11},{9,8},{10,9... | collective-permute-start | bytes 884744 | tf_op jit(solution)/shard_map/ppermute | solution.py:21
  5.1 18.7 %collective-permute-start.1 = (s32[1,48]{1,0:T(1,128)}, s32[1,48]{1,0:T(1,128)S(1)}, u32[]{:S(2)}, u32[]{:S(2)}) collective-permute-start(s32[1,48]{1,0:T(1,128)} %param.15), channel_id=1, source_target_pairs={{0,3},{1,0},{2,1},{3,2},{4,7},{5,4},{6,5},{7,6},{8,11},{9,8},{10,9... | collective-permute-start | bytes 584 | tf_op jit(solution)/shard_map/ppermute | solution.py:21
  8.5 2.4 %copy-start.10 = (bf16[256,384]{1,0:T(8,128)(2,1)}, bf16[256,384]{1,0:T(8,128)(2,1)S(1)}, u32[]{:S(2)}) copy-start(bf16[256,384]{1,0:T(8,128)(2,1)S(1)} %convolution_convert_fusion.11) | copy-start | bytes 589828
  8.5 7.9 %collective-permute-start.2 = (bf16[240,384]{1,0:T(8,128)(2,1)S(1)}, bf16[240,384]{1,0:T(8,128)(2,1)S(1)}, u32[]{:S(2)}, u32[]{:S(2)}) collective-permute-start(bf16[240,384]{1,0:T(8,128)(2,1)S(1)} %slice.53), channel_id=1, source_target_pairs={{0,1},{1,2},{2,3},{3,0},{4,5},{5,6},{6,7},{7,4},{8,9},{9,10},{10,1... | collective-permute-start | bytes 552968 | tf_op jit(solution)/shard_map/ppermute | solution.py:21
  10.9 9.4 %copy-start.4 = (bf16[1,384,384]{2,1,0:T(8,128)(2,1)S(1)}, bf16[1,384,384]{2,1,0:T(8,128)(2,1)}, u32[]{:S(2)}) copy-start(bf16[1,384,384]{2,1,0:T(8,128)(2,1)} %param.13) | copy-start | bytes 884740
  11.0 23.6 %copy-start.5 = (bf16[256,384]{1,0:T(8,128)(2,1)}, bf16[256,384]{1,0:T(8,128)(2,1)S(1)}, u32[]{:S(2)}) copy-start(bf16[256,384]{1,0:T(8,128)(2,1)S(1)} %fusion.31) | copy-start | bytes 589828
  23.8 0.7 copy-start.11
  26.0 1.5 copy-start.8
  37.8 19.0 %all-to-all-start = ((bf16[8,8,16,384]{3,2,1,0:T(8,128)(2,1)}), bf16[8,8,16,384]{3,2,1,0:T(8,128)(2,1)S(1)}, u32[]{:S(2)}, u32[]{:S(2)}) async-start(bf16[8,8,16,384]{3,2,1,0:T(8,128)(2,1)} %bitcast.195), calls=%async_computation | async-start | bytes 1572864 | tf_op jit(solution)/shard_map/all_to_all | solution.py:105
  41.5 11.1 %copy-start.6 = (bf16[256,384]{1,0:T(8,128)(2,1)S(1)}, bf16[256,384]{1,0:T(8,128)(2,1)}, u32[]{:S(2)}) copy-start(bf16[256,384]{1,0:T(8,128)(2,1)} %copy-done.5) | copy-start | bytes 589828
  41.5 11.1 %copy-start.9 = (bf16[1,384,384]{2,1,0:T(8,128)(2,1)S(1)}, bf16[1,384,384]{2,1,0:T(8,128)(2,1)}, u32[]{:S(2)}) copy-start(bf16[1,384,384]{2,1,0:T(8,128)(2,1)} %param.12) | copy-start | bytes 884740
  43.9 22.5 %collective-permute-start.3 = (bf16[8,128,384]{2,1,0:T(8,128)(2,1)}, bf16[8,128,384]{2,1,0:T(8,128)(2,1)}, u32[]{:S(2)}, u32[]{:S(2)}) collective-permute-start(bf16[8,128,384]{2,1,0:T(8,128)(2,1)} %fusion.3), channel_id=1, source_target_pairs={{0,1},{1,2},{2,3},{3,0},{4,5},{5,6},{6,7},{7,4},{8,9},{9,10},{10,1... | collective-permute-start | bytes 2359304 | tf_op jit(solution)/shard_map/ppermute | solution.py:21
  45.6 37.7 %collective-permute-start.4 = (bf16[8,128,384]{2,1,0:T(8,128)(2,1)}, bf16[8,128,384]{2,1,0:T(8,128)(2,1)}, u32[]{:S(2)}, u32[]{:S(2)}) collective-permute-start(bf16[8,128,384]{2,1,0:T(8,128)(2,1)} %add_convert_fusion.3), channel_id=1, source_target_pairs={{0,3},{1,0},{2,1},{3,2},{4,7},{5,4},{6,5},{7,6},{8,11},{9,8},{10,9... | collective-permute-start | bytes 2359304 | tf_op jit(solution)/shard_map/ppermute | solution.py:21
  48.8 52.4 %collective-permute-start.5 = (bf16[8,112,384]{2,1,0:T(8,128)(2,1)}, bf16[8,112,384]{2,1,0:T(8,128)(2,1)}, u32[]{:S(2)}, u32[]{:S(2)}) collective-permute-start(bf16[8,112,384]{2,1,0:T(8,128)(2,1)} %fusion.11), channel_id=1, source_target_pairs={{0,1},{1,2},{2,3},{3,0},{4,5},{5,6},{6,7},{7,4},{8,9},{9,10},{10,1... | collective-permute-start | bytes 2064392 | tf_op jit(solution)/shard_map/ppermute | solution.py:21
  48.8 63.2 %collective-permute-start.6 = (bf16[8,112,384]{2,1,0:T(8,128)(2,1)}, bf16[8,112,384]{2,1,0:T(8,128)(2,1)}, u32[]{:S(2)}, u32[]{:S(2)}) collective-permute-start(bf16[8,112,384]{2,1,0:T(8,128)(2,1)} %fusion.2), channel_id=1, source_target_pairs={{0,3},{1,0},{2,1},{3,2},{4,7},{5,4},{6,5},{7,6},{8,11},{9,8},{10,9... | collective-permute-start | bytes 2064392 | tf_op jit(solution)/shard_map/ppermute | solution.py:21
  56.8 33.2 %all-to-all-start.1 = ((bf16[8,8,16,384]{3,2,1,0:T(8,128)(2,1)}), bf16[8,8,16,384]{3,2,1,0:T(8,128)(2,1)}, u32[]{:S(2)}, u32[]{:S(2)}) async-start(bf16[8,8,16,384]{3,2,1,0:T(8,128)(2,1)} %bitcast.194), calls=%async_computation.1 | async-start | bytes 1572864 | tf_op jit(solution)/shard_map/all_to_all | solution.py:105
  90.0 21.9 %all-to-all-start.2 = ((bf16[8,8,16,384]{3,2,1,0:T(8,128)(2,1)}), bf16[8,8,16,384]{3,2,1,0:T(8,128)(2,1)}, u32[]{:S(2)}, u32[]{:S(2)}) async-start(bf16[8,8,16,384]{3,2,1,0:T(8,128)(2,1)} %bitcast.196), calls=%async_computation.2 | async-start | bytes 1572864 | tf_op jit(solution)/shard_map/all_to_all | solution.py:105
  118.6 16.8 %all-to-all-start.3 = ((bf16[8,8,16,384]{3,2,1,0:T(8,128)(2,1)}), bf16[8,8,16,384]{3,2,1,0:T(8,128)(2,1)}, u32[]{:S(2)}, u32[]{:S(2)}) async-start(bf16[8,8,16,384]{3,2,1,0:T(8,128)(2,1)} %bitcast.197), calls=%async_computation.3 | async-start | bytes 1572864 | tf_op jit(solution)/shard_map/all_to_all | solution.py:105
  122.8 1.6 copy-start.2
  129.7 0.9 copy-start.1
  135.4 16.1 %all-to-all-start.4 = ((bf16[8,8,16,384]{3,2,1,0:T(8,128)(2,1)}), bf16[8,8,16,384]{3,2,1,0:T(8,128)(2,1)S(1)}, u32[]{:S(2)}, u32[]{:S(2)}) async-start(bf16[8,8,16,384]{3,2,1,0:T(8,128)(2,1)} %bitcast.184), calls=%async_computation.4 | async-start | bytes 1572864 | tf_op jit(solution)/shard_map/all_to_all | solution.py:105
  139.0 1.6 copy-start.3
  147.1 8.8 %copy-start.7 = (bf16[256,384]{1,0:T(8,128)(2,1)S(1)}, bf16[256,384]{1,0:T(8,128)(2,1)}, u32[]{:S(2)}) copy-start(bf16[256,384]{1,0:T(8,128)(2,1)} %copy-done.5) | copy-start | bytes 589828
  151.5 16.8 %all-to-all-start.5 = ((bf16[8,8,16,384]{3,2,1,0:T(8,128)(2,1)}), bf16[8,8,16,384]{3,2,1,0:T(8,128)(2,1)}, u32[]{:S(2)}, u32[]{:S(2)}) async-start(bf16[8,8,16,384]{3,2,1,0:T(8,128)(2,1)} %bitcast.48), calls=%async_computation.5 | async-start | bytes 1572864 | tf_op jit(solution)/shard_map/all_to_all | solution.py:105
